TPU v7x, 512 devices: a whole 4x4x16 slice. The times are simulated.
512 devices in a mesh: seq: 64 (over z_hi, x, y), sub: 8 (over z_lo, core).
Axes of the slice: x: 4, y: 4, z: 16 (z_hi: 4, z_lo: 4; z = z_hi * 4 + z_lo), core: 2. Of those that a mesh axis runs over, the one named last changes fastest.
Arguments:
- queries: bfloat16 [32768, 2048], P('seq', 'sub'), may hold values from -6 to 6, as said below
- keys: bfloat16 [32768, 2048], P('seq', 'sub'), may hold values from -6 to 6
- values: bfloat16 [32768, 2048], P('seq', 'sub'), may hold values from -6 to 6
- offsets: int32 [32768], P('seq'), may hold values from 1 to 64
- negatives: int32 [32768, 15], P('seq'), may hold values from 0 to 511
Outputs:
- grad_queries: bfloat16 [32768, 2048], P('seq', 'sub')
- grad_keys: bfloat16 [32768, 2048], P('seq', 'sub')
- grad_values: bfloat16 [32768, 2048], P('seq', 'sub')
- loss: float32 [], replicated
Inputs may be any that keep to these rules, and one draw needn't show every extreme that they name: `queries`: some rows may be closely aligned with the keys they see, giving scores of several hundred. `offsets`: the positive sample of step t is step (t + value) mod 32768.
All inputs are finite; a program needn't handle non-finite values.
Results may differ from a plain program's by a relative error of at most 0.029.
Values may be sent and summed in bfloat16 or wider, within the bound.
A program may use at most 64 MiB of HBM per device.

v0:
```python
import math

import jax
import jax.numpy as jnp
from jax import lax
from jax.sharding import PartitionSpec as P

DH = 128
D = 2048
BLOCK = 512
STRIDE = 64
OFFMAX = 64


EPSILON = 1e-05
TEMPER = 0.1
MASKED = -1e30


def from_behind(x, axis, by):
    devices = lax.axis_size(axis)
    return lax.ppermute(x, axis, [(i, (i + by) % devices) for i in range(devices)])


def block_probs(query_blk, keys_all, allowed, scaling):
    scores = (
        jnp.einsum("qhe,khe->hqk", query_blk, keys_all, preferred_element_type=jnp.float32)
        * scaling
    )
    highest = jnp.max(jnp.where(allowed, scores, MASKED), axis=2, keepdims=True)
    summed = jnp.sum(jnp.where(allowed, jnp.exp(scores - highest), 0.0), axis=2, keepdims=True)
    log_total = highest + jnp.log(summed)
    return jnp.where(allowed, jnp.exp(scores - log_total), 0.0).astype(jnp.bfloat16)


def contrast(positive, negative, squares, target, picked, weight, extended):
    row_count = positive.shape[0]
    ext_count = extended.shape[0]
    radius = jnp.sqrt(squares / D + EPSILON)
    own_radius = radius[:row_count]
    first_factor = 1.0 / (D * TEMPER * own_radius * radius[target])
    rest_factor = 1.0 / (D * TEMPER * own_radius[:, None] * radius[picked])
    first_logit = positive * first_factor
    rest_logit = negative * rest_factor
    logits = jnp.concatenate([first_logit[:, None], rest_logit], axis=1)
    expsum = jnp.sum(jnp.exp(logits), axis=1)
    loss_part = jnp.sum(weight * (jnp.log(expsum) - first_logit))
    chosen_mark = (jnp.arange(logits.shape[1], dtype=jnp.int32) == 0).astype(jnp.float32)
    grad_logit = (jnp.exp(logits) / expsum[:, None] - chosen_mark[None, :]) * weight[:, None]
    grad_first = grad_logit[:, 0] * first_factor
    grad_rest = grad_logit[:, 1:] * rest_factor
    all_columns = jnp.concatenate([target[:, None], picked], axis=1)
    pair_coeffs = jnp.concatenate([grad_first[:, None], grad_rest], axis=1)
    radius_coeffs = jnp.concatenate(
        [
            (-grad_logit[:, 0] * first_logit / radius[target])[:, None],
            -grad_logit[:, 1:] * rest_logit / radius[picked],
        ],
        axis=1,
    )
    row_ids = jnp.broadcast_to(jnp.arange(row_count, dtype=jnp.int32)[:, None], all_columns.shape)
    pair_table = (
        jnp.zeros((row_count, ext_count), jnp.float32).at[row_ids, all_columns].add(pair_coeffs)
    )
    wide_rows = extended.astype(jnp.float32)
    own_rows = wide_rows[:row_count]
    pulled = jnp.dot(
        pair_table, wide_rows, precision=lax.Precision.HIGHEST, preferred_element_type=jnp.float32
    )
    pushed = jnp.dot(
        pair_table.T, own_rows, precision=lax.Precision.HIGHEST, preferred_element_type=jnp.float32
    )
    grad_ext = pushed.at[:row_count].add(pulled)
    grad_radius = jnp.zeros((ext_count,), jnp.float32).at[all_columns].add(radius_coeffs)
    grad_radius = grad_radius.at[:row_count].add(-jnp.sum(grad_logit * logits, axis=1) / own_radius)
    return (loss_part, grad_ext, grad_radius)


def local(queries, keys, values, offsets, negatives):
    row_count, feat_count = queries.shape
    head_count = feat_count // DH
    scaling = 1.0 / math.sqrt(DH)
    seq_count = lax.axis_size("seq")
    token_total = row_count * seq_count
    first_row = lax.axis_index("seq") * row_count
    summary_k = keys[STRIDE - 1 :: STRIDE]
    summary_v = values[STRIDE - 1 :: STRIDE]
    panel_k, panel_v = (
        lax.all_gather(summary_k, "seq", axis=0, tiled=True),
        lax.all_gather(summary_v, "seq", axis=0, tiled=True),
    )
    panel_count = panel_k.shape[0]
    panel_pos = jnp.arange(panel_count, dtype=jnp.int32) * STRIDE + (STRIDE - 1)
    query_h = queries.reshape(row_count, head_count, DH)
    key_h = keys.reshape(row_count, head_count, DH)
    value_h = values.reshape(row_count, head_count, DH)
    panel_kh = panel_k.reshape(panel_count, head_count, DH)
    panel_vh = panel_v.reshape(panel_count, head_count, DH)
    within = jnp.arange(BLOCK, dtype=jnp.int32)
    causal = within[:, None] >= within[None, :]
    block_start = 0
    reachable = panel_pos < first_row + block_start
    allowed = jnp.concatenate(
        [causal, jnp.broadcast_to(reachable[None, :], (BLOCK, panel_count))], axis=1
    )[None]
    keys_all = jnp.concatenate([key_h, panel_kh], axis=0)
    values_all = jnp.concatenate([value_h, panel_vh], axis=0)
    windows = [(block_start, allowed, keys_all, values_all)]
    block_start, allowed, keys_all, values_all = windows[0]
    soft_weights = block_probs(query_h, keys_all, allowed, scaling)
    kept_probs = [soft_weights]
    mixture = jnp.einsum(
        "hqk,khe->qhe", soft_weights, values_all, preferred_element_type=jnp.float32
    )
    outputs = mixture.reshape(BLOCK, feat_count).astype(jnp.bfloat16)
    ahead_rows = from_behind(outputs[:OFFMAX], "seq", -1)
    extended = jnp.concatenate([outputs, ahead_rows], axis=0)
    gram_rows = jnp.einsum("rf,cf->rc", outputs, extended, preferred_element_type=jnp.float32)
    wide_rows = extended.astype(jnp.float32)
    local_rows = jnp.arange(row_count, dtype=jnp.int32)
    target = local_rows + offsets
    squares, positive, negative = (
        lax.psum(jnp.sum(wide_rows * wide_rows, axis=1).astype(jnp.bfloat16), "sub").astype(
            jnp.float32
        ),
        lax.psum(gram_rows[local_rows, target].astype(jnp.bfloat16), "sub").astype(jnp.float32),
        lax.psum(gram_rows[local_rows[:, None], negatives].astype(jnp.bfloat16), "sub").astype(
            jnp.float32
        ),
    )
    weight = (1.0 + 2.0 * (first_row + local_rows).astype(jnp.float32) / token_total) / token_total
    loss_part, grad_ext, grad_radius = contrast(
        positive, negative, squares, target, negatives, weight, extended
    )
    loss_value = lax.psum(loss_part, "seq")
    tail_grad, tail_radius = (
        from_behind(grad_ext[row_count:].astype(jnp.bfloat16), "seq", 1).astype(jnp.float32),
        from_behind(grad_radius[row_count:].astype(jnp.bfloat16), "seq", 1).astype(jnp.float32),
    )
    grad_main = grad_ext[:row_count].at[:OFFMAX].add(tail_grad)
    radius_main = grad_radius[:row_count].at[:OFFMAX].add(tail_radius)
    own_radius = jnp.sqrt(squares[:row_count] / D + EPSILON)
    grad_att = grad_main + (radius_main / (D * own_radius))[:, None] * wide_rows[:row_count]
    grad_out = grad_att.astype(jnp.bfloat16)
    grad_out_h = grad_out.reshape(row_count, head_count, DH)
    attended_h = outputs.reshape(row_count, head_count, DH)
    query_parts, key_parts, value_parts = ([], [], [])
    panel_term = jnp.zeros((panel_count, 2 * feat_count), jnp.float32)
    for window, soft_weights in zip(windows, kept_probs):
        block_start, allowed, keys_all, values_all = window
        grad_prob = jnp.einsum(
            "qhe,khe->hqk", grad_out_h, values_all, preferred_element_type=jnp.float32
        )
        delta_rows = jnp.sum(
            grad_out_h.astype(jnp.float32) * attended_h.astype(jnp.float32), axis=2
        )
        grad_score = (
            soft_weights.astype(jnp.float32) * (grad_prob - jnp.transpose(delta_rows)[:, :, None])
        ).astype(jnp.bfloat16)
        grad_query = (
            jnp.einsum("hqk,khe->qhe", grad_score, keys_all, preferred_element_type=jnp.float32)
            * scaling
        )
        query_parts.append(grad_query.reshape(BLOCK, feat_count).astype(jnp.bfloat16))
        near_key = (
            jnp.einsum(
                "hqk,qhe->khe",
                grad_score[:, :, :BLOCK],
                query_h,
                preferred_element_type=jnp.float32,
            )
            * scaling
        )
        near_value = jnp.einsum(
            "hqk,qhe->khe",
            soft_weights[:, :, :BLOCK],
            grad_out_h,
            preferred_element_type=jnp.float32,
        )
        key_parts.append(near_key.reshape(BLOCK, feat_count))
        value_parts.append(near_value.reshape(BLOCK, feat_count))
        panel_key = (
            jnp.einsum(
                "hqk,qhe->khe",
                grad_score[:, :, BLOCK:],
                query_h,
                preferred_element_type=jnp.float32,
            )
            * scaling
        )
        panel_value = jnp.einsum(
            "hqk,qhe->khe",
            soft_weights[:, :, BLOCK:],
            grad_out_h,
            preferred_element_type=jnp.float32,
        )
        panel_term = jnp.concatenate(
            [
                panel_key.reshape(panel_count, feat_count),
                panel_value.reshape(panel_count, feat_count),
            ],
            axis=1,
        )
    slice_rows = row_count // STRIDE
    own_term = lax.psum_scatter(panel_term, "seq", scatter_dimension=0, tiled=True)
    grad_queries = query_parts[0]
    grad_keys = (
        key_parts[0]
        .reshape(slice_rows, STRIDE, feat_count)
        .at[:, STRIDE - 1]
        .add(own_term[:, :feat_count])
    )
    grad_values = (
        value_parts[0]
        .reshape(slice_rows, STRIDE, feat_count)
        .at[:, STRIDE - 1]
        .add(own_term[:, feat_count:])
    )
    return (
        grad_queries,
        grad_keys.reshape(row_count, feat_count).astype(jnp.bfloat16),
        grad_values.reshape(row_count, feat_count).astype(jnp.bfloat16),
        loss_value,
    )


def solution(mesh):
    placed = (P("seq", "sub"), P("seq", "sub"), P("seq", "sub"), P("seq"), P("seq", None))
    return jax.shard_map(
        local,
        mesh=mesh,
        in_specs=placed,
        out_specs=(P("seq", "sub"), P("seq", "sub"), P("seq", "sub"), P()),
        check_vma=False,
    )
```

profile of v0, /device:TPU:32, one launch (start us, length us, event | category | flops | bytes accessed | tf_op | source)
XLA Modules:
  0.0 1178.9 jit_solution(2600753398353093522)
XLA Ops:
  8.3 1.1 copy.109
  10.4 1.1 copy.115
  11.5 1.2 copy.157
  12.7 228.4 %all_gather.6 = bf16[512,256]{1,0:T(8,128)(2,1)S(1)} all-gather(bf16[8,256]{1,0:T(8,128)(2,1)S(1)} %slice.168), channel_id=1, replica_groups=mesh['seq'=64,'sub'=8] {'seq'}, dimensions={0}, use_global_device_ids=true | all-gather | bytes 266240 | tf_op jit(solution)/shard_map/all_gather | solution.py:89
  243.9 1.1 fusion.6
  244.9 213.8 %all_gather.7 = bf16[512,256]{1,0:T(8,128)(2,1)S(1)} all-gather(bf16[8,256]{1,0:T(8,128)(2,1)S(1)} %slice.169), channel_id=1, replica_groups=mesh['seq'=64,'sub'=8] {'seq'}, dimensions={0}, use_global_device_ids=true | all-gather | bytes 266240 | tf_op jit(solution)/shard_map/all_gather | solution.py:90
  459.5 3.9 collective-permute-start
  466.7 4.8 gather_fusion
  471.5 64.5 %gather_fusion.2 = bf16[7680]{0:T(1024)(128)(2,1)S(1)} fusion(bf16[512,576]{0,1:T(8,128)(2,1)S(1)} %fusion.30, s32[7680]{0:T(1024)S(1)} %reshape.348), kind=kCustom, calls=%fused_computation.2 | custom fusion | bytes 92160 | tf_op jit(solution)/shard_map/gather | solution.py:127
  536.4 24.5 %all-reduce = (bf16[512,15]{1,0:T(8,128)(2,1)S(1)}, bf16[576]{0:T(1024)(128)(2,1)S(1)}, bf16[512]{0:T(512)(128)(2,1)S(1)}) all-reduce(bf16[512,15]{1,0:T(8,128)(2,1)S(1)} %reshape.380, bf16[576]{0:T(1024)(128)(2,1)S(1)} %multiply_reduce_fusion, bf16[512]{0:T(512)(128)(2,1)S(1)} %gather_fusion), channel_id=1, replica_groups=mesh['seq'=64,'sub'=8] {'sub'}, use_global_device_ids=true, to_apply=%region_5.6 | all-reduce | flops 8768 | bytes 35072 | tf_op jit(solution)/shard_map/psum | solution.py:127
  560.9 2.3 gather_fusion.1
  563.2 27.1 %gather_fusion.3 = f32[7680]{0:T(1024)S(1)} fusion(f32[576]{0:T(1024)S(1)} %add_sqrt_fusion, s32[8192]{0:T(1024)S(1)} %pad_clamp_fusion), kind=kCustom, calls=%fused_computation.3 | custom fusion | bytes 92160 | tf_op jit(solution)/shard_map/gather | solution.py:42
  592.4 1.3 multiply_reduce_fusion.4
  594.2 57.2 %scatter_custom_fusion = f32[576]{0:T(1024)S(1)} fusion(s32[8192]{0:T(1024)} %reshape.364, f32[8192]{0:T(1024)S(1)} %reshape.366, f32[]{:T(128)} %constant.190.clone.1), kind=kCustom, calls=%fused_computation.80 | custom fusion | flops 8192 | bytes 2816 | tf_op jit(solution)/shard_map/scatter-add | solution.py:74
  652.0 3.0 collective-permute-start.2
  654.9 1.2 divide_add_fusion
  656.6 44.4 %scatter_custom_fusion.1 = f32[294912]{0:T(1024)} fusion(s32[8192]{0:T(1024)} %reshape.370, f32[8192]{0:T(1024)S(1)} %reshape.372, f32[]{:T(128)} %constant.190.clone.1), kind=kCustom, calls=%fused_computation.34 | custom fusion | flops 8192 | bytes 1180160
  701.0 1.5 reshape.332
  702.5 1.6 fusion.31
  704.1 3.0 collective-permute-start.1
  707.2 2.0 convolution_add_fusion
  709.9 8.6 collective-permute-done.1
  718.8 1.0 multiply_reduce_fusion.1
  720.5 1.8 multiply_convert_fusion
  722.4 1.3 copy-done.1
  723.7 1.2 fusion.7
  724.9 1.2 copy.137
  727.2 2.2 pad_maximum_fusion
  729.4 216.4 %psum.31 = f32[]{:T(128)} all-reduce(f32[]{:T(128)} %get-tuple-element.103), channel_id=1, replica_groups=mesh['seq'=64,'sub'=8] {'seq'}, use_global_device_ids=true, to_apply=%region_13.14 | all-reduce | flops 1 | bytes 8 | tf_op jit(solution)/shard_map/psum | solution.py:135
  946.9 1.7 fusion.8
  949.5 2.2 fusion.9
  952.5 216.5 %reduce-scatter.2.cloned.1.call-done = f32[8,512]{1,0:T(8,128)} async-done(((f32[512,512]{1,0:T(8,128)}), f32[8,512]{1,0:T(8,128)}) %reduce-scatter.2.cloned.1.call-update) | async-done | bytes 16400 | tf_op jit(solution)/shard_map/reduce_scatter | solution.py:205
  (127 shorter events, 21.0 us)
Async XLA Ops:
  7.2 1161.8 %reduce-scatter.2.cloned.1.call-start = ((), (), s32[]{:S(2)}) async-start(), calls=%async_computation.1 | async-start | bytes 1064960 | tf_op jit(solution)/shard_map/reduce_scatter | solution.py:205
  11.5 447.5 %copy-start.2 = (bf16[512,256]{0,1:T(8,128)(2,1)}, bf16[512,256]{0,1:T(8,128)(2,1)S(1)}, u32[]{:S(2)}) copy-start(bf16[512,256]{0,1:T(8,128)(2,1)S(1)} %copy.115) | copy-start | bytes 786436
  12.7 230.1 %copy-start.9 = (bf16[512,256]{0,1:T(8,128)(2,1)}, bf16[512,256]{0,1:T(8,128)(2,1)S(1)}, u32[]{:S(2)}) copy-start(bf16[512,256]{0,1:T(8,128)(2,1)S(1)} %copy.157) | copy-start | bytes 786436
  241.4 2.4 copy-start.7
  241.5 2.2 copy-start.12
  243.8 219.6 %copy-start.6 = (s32[512,15]{0,1:T(8,128)S(1)}, s32[512,15]{0,1:T(8,128)}, u32[]{:S(2)}) copy-start(s32[512,15]{0,1:T(8,128)} %param.21) | copy-start | bytes 92164
  243.8 219.6 %copy-start.17 = (s32[512]{0:T(512)S(1)}, s32[512]{0:T(512)}, u32[]{:S(2)}) copy-start(s32[512]{0:T(512)} %param.20) | copy-start | bytes 6148
  243.8 220.1 %copy-start.19 = (s32[2]{0:T(128)S(1)}, s32[2]{0:T(128)}, u32[]{:S(2)}) copy-start(s32[2]{0:T(128)} %constant.200) | copy-start | bytes 28
  243.8 220.2 %copy-start.18 = (s32[2]{0:T(128)S(1)}, s32[2]{0:T(128)}, u32[]{:S(2)}) copy-start(s32[2]{0:T(128)} %constant.203) | copy-start | bytes 28
  458.9 4.6 copy-start.3
  459.4 76.6 %copy-start = (bf16[2,128,512]{2,1,0:T(8,128)(2,1)}, bf16[2,128,512]{2,1,0:T(8,128)(2,1)S(1)}, u32[]{:S(2)}) copy-start(bf16[2,128,512]{2,1,0:T(8,128)(2,1)S(1)} %convolution_convert_fusion) | copy-start | bytes 786436
  459.5 6.9 collective-permute-start
  466.4 69.9 %copy-start.4 = (bf16[64,256]{1,0:T(8,128)(2,1)}, bf16[64,256]{1,0:T(8,128)(2,1)S(1)}, u32[]{:S(2)}) copy-start(bf16[64,256]{1,0:T(8,128)(2,1)S(1)} %collective-permute-done) | copy-start | bytes 98308
  560.9 29.4 %copy-start.14 = (bf16[576]{0:T(1024)(128)(2,1)}, bf16[576]{0:T(1024)(128)(2,1)S(1)}, u32[]{:S(2)}) copy-start(bf16[576]{0:T(1024)(128)(2,1)S(1)} %get-tuple-element.93) | copy-start | bytes 3460
  590.6 1.5 copy-start.13
  652.0 57.3 %collective-permute-start.2 = (bf16[64]{0:T(256)(128)(2,1)}, bf16[64]{0:T(256)(128)(2,1)}, u32[]{:S(2)}, u32[]{:S(2)}) collective-permute-start(bf16[64]{0:T(256)(128)(2,1)} %slice.180), channel_id=1, source_target_pairs={{0,8},{8,16},{16,24},{24,32},{32,40},{40,48},{48,56},{56,64},{64,7... | collective-permute-start | bytes 392 | tf_op jit(solution)/shard_map/ppermute | solution.py:22
  701.0 8.2 copy-start.15
  701.0 8.3 copy-start.16
  702.5 6.7 copy-start.5
  704.1 14.3 %collective-permute-start.1 = (bf16[64,256]{1,0:T(8,128)(2,1)S(1)}, bf16[64,256]{1,0:T(8,128)(2,1)S(1)}, u32[]{:S(2)}, u32[]{:S(2)}) collective-permute-start(bf16[64,256]{1,0:T(8,128)(2,1)S(1)} %slice.250), channel_id=1, source_target_pairs={{0,8},{8,16},{16,24},{24,32},{32,40},{40,48},{48,56},{56,64},{64,7... | collective-permute-start | bytes 98312 | tf_op jit(solution)/shard_map/ppermute | solution.py:22
  720.5 3.2 copy-start.10
  722.4 1.4 copy-start.1
  729.4 217.6 %copy-start.11 = (bf16[512,256]{0,1:T(8,128)(2,1)S(1)}, bf16[512,256]{0,1:T(8,128)(2,1)}, u32[]{:S(2)}) copy-start(bf16[512,256]{0,1:T(8,128)(2,1)} %copy-done.9) | copy-start | bytes 786436
  729.4 220.1 %copy-start.8 = (bf16[512,2,128]{2,0,1:T(8,128)(2,1)S(1)}, bf16[512,2,128]{2,0,1:T(8,128)(2,1)}, u32[]{:S(2)}) copy-start(bf16[512,2,128]{2,0,1:T(8,128)(2,1)} %copy-done.7) | copy-start | bytes 786436
Sparse Core Ops, SparseCore 0:
  729.5 439.4 reduce-scatter.1
where the time goes:
time: 1180 us
  blocking collectives  683 us (58%)
  waiting for transfers between devices  225 us (19%)
  local copies, waits for them, and re-layouts  118 us (10%)
  other arithmetic  115 us (10%)
  between operations  14.9 us (1%)
  matrix products  13.1 us (1%)
    all_gather x1, blocking collectives, local(): lax.all_gather(summary_k, 'seq', axis=0, tiled=True)  228 us
    reduce_scatter x1, waiting for transfers between devices, local(): lax.psum_scatter(panel_term, 'seq', scatter_dimension=0, tiled=True)  216 us
    psum x1, blocking collectives, local(): loss_value = lax.psum(loss_part, 'seq')  216 us
    all_gather x1, blocking collectives, local(): lax.all_gather(summary_v, 'seq', axis=0, tiled=True)  214 us
    gather x1, local copies, waits for them, and re-layouts, local(): gram_rows[local_rows[:, None], negatives].astype(jnp.bfloat16)  64.5 us
    scatter-add x1, other arithmetic, contrast(): jnp.zeros((ext_count,), jnp.float32).at[all_columns].add(radius_coeffs)  57.2 us
    unnamed x4, other arithmetic  44.6 us
    gather x2, local copies, waits for them, and re-layouts, contrast(): rest_factor = 1.0 / (D * TEMPER * own_radius[:, None] * radius[picked])  27.3 us
  transfers between devices with their start and end apart: 4, of which 2 were waited for; matrix products, arithmetic and copies ran while one was open for 5% of the time, Pallas kernels for 0%

commit v1 on v0

v1 whole, which is shorter than its diff:
```python
import math

import jax
import jax.numpy as jnp
from jax import lax
from jax.experimental import pallas as pl
from jax.experimental.pallas import tpu as pltpu
from jax.sharding import PartitionSpec as P

DH = 128
D = 2048
ROWS = 512
FEAT = 256
STRIDE = 64
OFFMAX = 64
NZ = 4
NXY = 16
NSUB = 8
NSEQ = 64
TOKENS = 32768
PANEL = 1024

EPSILON = 1e-05
TEMPER = 0.1
MASKED = -1e30
SCALE = 1.0 / math.sqrt(DH)
SCALE2 = SCALE * math.log2(math.e)

F32 = jnp.float32
BF16 = jnp.bfloat16
I32 = jnp.int32
MESH = pl.DeviceIdType.MESH


def nn(a, b):
    return lax.dot_general(a, b, (((1,), (0,)), ((), ())), preferred_element_type=F32)


def nt(a, b):
    return lax.dot_general(a, b, (((1,), (1,)), ((), ())), preferred_element_type=F32)


def tn(a, b):
    return lax.dot_general(a, b, (((0,), (0,)), ((), ())), preferred_element_type=F32)


def iota(shape, dim):
    return lax.broadcasted_iota(I32, shape, dim)


def pick_lanes(x, index):
    return jnp.take_along_axis(x, index, axis=1, mode="promise_in_bounds")


def split(x):
    high = x.astype(BF16)
    return high, (x - high.astype(F32)).astype(BF16)


def kernel(
    q_ref, k_ref, v_ref, off_ref, neg_ref,
    dq_ref, dk_ref, dv_ref, loss_ref,
    gat, kblk, vblk, kblk_t, vblk_t, k_t, v_t, s_scr, p1, p2, o1, att, att_t, ahead,
    idx, idx_t, picked, pk_buf, sq_buf, coef, rcoef, ct_hi, ct_lo, h_hi, h_lo, grad_t,
    tail_out, tail_in, loss_xy, loss_z, gm, rs, rz_out, rz, dk_acc, dv_acc,
    z_sem, xy_sem, near_sem, pk_sem, sq_sem, lxy_sem, lz_sem, rs_sem, rz_sem,
):
    seq = lax.axis_index("seq").astype(I32)
    sub = lax.axis_index("sub").astype(I32)
    z, xy = lax.div(seq, NXY), lax.rem(seq, NXY)
    nxt, prv = lax.rem(seq + 1, NSEQ), lax.rem(seq + NSEQ - 1, NSEQ)

    def z_peer(j):
        return lax.rem(z + j, NZ) * NXY + xy

    def xy_peer(j):
        return z * NXY + lax.rem(xy + j, NXY)

    def sub_peer(j):
        return lax.rem(sub + j, NSUB)

    def remote(src, dst, sems, j, to_seq, to_sub):
        return pltpu.make_async_remote_copy(
            src_ref=src, dst_ref=dst, send_sem=sems.at[0, j], recv_sem=sems.at[1, j],
            device_id=(to_seq, to_sub), device_id_type=MESH,
        )

    def each(count, make, act):
        def body(j, carry):
            act(make(j))
            return carry

        lax.fori_loop(1, count, body, 0)

    def start(copy):
        copy.start()

    def finish(copy):
        copy.wait()

    barrier = pltpu.get_barrier_semaphore()

    def greet(to_seq, to_sub):
        pl.semaphore_signal(barrier, inc=1, device_id=(to_seq, to_sub), device_id_type=MESH)

    each(NZ, z_peer, lambda s: greet(s, sub))
    each(NXY, xy_peer, lambda s: greet(s, sub))
    each(NSUB, sub_peer, lambda u: greet(seq, u))
    greet(nxt, sub)
    greet(prv, sub)

    own_row = pl.multiple_of((xy * NZ + z) * 16, 16)
    chosen = (iota((16, ROWS), 1) == (iota((16, ROWS), 0) & 7) * STRIDE + (STRIDE - 1)).astype(F32).astype(BF16)
    first8 = iota((16, DH), 0) < 8
    k_sel = nn(chosen, k_ref[...])
    v_sel = nn(chosen, v_ref[...])
    gat[pl.ds(own_row, 16), :] = jnp.concatenate(
        [
            jnp.where(first8, k_sel[:, :DH], k_sel[:, DH:]),
            jnp.where(first8, v_sel[:, :DH], v_sel[:, DH:]),
        ],
        axis=1,
    ).astype(BF16)
    ahead[OFFMAX:, :] = jnp.zeros((128 - OFFMAX, FEAT), BF16)
    tail_in[OFFMAX:, :] = jnp.zeros((128 - OFFMAX, FEAT), BF16)

    pl.semaphore_wait(barrier, (NZ - 1) + (NXY - 1) + (NSUB - 1) + 2)

    def z_copy(j):
        tile = gat.at[pl.ds(own_row, 16), :]
        return remote(tile, tile, z_sem, j, z_peer(j), sub)

    block_row = pl.multiple_of(xy * 64, 64)

    def xy_copy(j):
        block = gat.at[pl.ds(block_row, 64), :]
        return remote(block, block, xy_sem, j, xy_peer(j), sub)

    each(NZ, z_copy, start)
    k_t[...] = k_ref[...].T
    v_t[...] = v_ref[...].T
    each(NZ, z_copy, finish)
    each(NXY, xy_copy, start)

    idx[...] = jnp.zeros((ROWS, 128), I32)
    idx[:, 0:15] = neg_ref[...]
    for b in range(4):
        rows = slice(b * 128, (b + 1) * 128)
        shift = jnp.broadcast_to(off_ref[b : b + 1, :], (128, 128)).T
        target = shift + iota((128, 128), 0) + b * 128
        both = jnp.where(iota((128, 128), 1) == 15, target, idx[rows, :])
        idx[rows, :] = both
        idx_t[:, rows] = both.T[0:16, :]

    lane_q = iota((64, ROWS), 1)
    row_k = iota((64, ROWS), 0)

    def rows64(i, base=0):
        return pl.ds(pl.multiple_of(base + i * 64, 64), 64)

    m1, l1 = [], []
    for h in range(2):
        cols = slice(h * DH, (h + 1) * DH)
        base = h * ROWS
        s_scr[base : base + ROWS, :] = nt(k_ref[:, cols], q_ref[:, cols])

        def top(i, best, base=base):
            x = s_scr[rows64(i, base), :]
            x = jnp.where(row_k + i * 64 <= lane_q, x, MASKED)
            s_scr[rows64(i, base), :] = x
            return jnp.maximum(best, jnp.max(x.reshape(8, 8, ROWS), axis=0))

        best = lax.fori_loop(0, 8, top, jnp.full((8, ROWS), MASKED, F32))
        level = jnp.max(best, axis=0, keepdims=True) * SCALE2

        def soft(i, total, base=base, level=level):
            p = jnp.exp2(s_scr[rows64(i, base), :] * SCALE2 - level)
            p1[rows64(i, base), :] = p.astype(BF16)
            return total + jnp.sum(p.reshape(8, 8, ROWS), axis=0)

        total = lax.fori_loop(0, 8, soft, jnp.zeros((8, ROWS), F32))
        m1.append(level)
        l1.append(jnp.sum(total, axis=0, keepdims=True))
        o1[cols, :] = nn(v_t[cols, :], p1[base : base + ROWS, :])

    each(NXY, xy_copy, finish)
    for b in range(4):
        rows = slice(b * 256, (b + 1) * 256)
        in_first = (iota((256, DH), 0) & 15) < 8
        one = jnp.where(in_first, 1.0, 0.0).astype(BF16)
        two = jnp.where(in_first, 0.0, 1.0).astype(BF16)
        in_first_t = (iota((DH, 256), 1) & 15) < 8
        one_t = jnp.where(in_first_t, 1.0, 0.0).astype(BF16)
        two_t = jnp.where(in_first_t, 0.0, 1.0).astype(BF16)
        for lanes, blk, blk_t in ((slice(0, DH), kblk, kblk_t), (slice(DH, FEAT), vblk, vblk_t)):
            tile = gat[rows, lanes]
            tile_t = tile.T
            blk[rows, 0:DH] = tile * one
            blk[rows, DH:FEAT] = tile * two
            blk_t[0:DH, rows] = tile_t * one_t
            blk_t[DH:FEAT, rows] = tile_t * two_t

    s_scr[...] = nt(kblk[...], q_ref[...])
    slot_z = lax.shift_right_logical(row_k, 4) * NXY

    def top2(i, best):
        x = s_scr[rows64(i), :]
        x = jnp.where(slot_z + i < seq, x, MASKED)
        s_scr[rows64(i), :] = x
        return jnp.maximum(best, jnp.max(x.reshape(4, 16, ROWS), axis=0))

    best = lax.fori_loop(0, NXY, top2, jnp.full((16, ROWS), MASKED, F32))
    m2 = [jnp.max(best[0:8], axis=0, keepdims=True) * SCALE2, jnp.max(best[8:16], axis=0, keepdims=True) * SCALE2]
    level16 = jnp.concatenate([jnp.broadcast_to(m2[0], (8, ROWS)), jnp.broadcast_to(m2[1], (8, ROWS))], axis=0)

    def soft2(i, total):
        p = jnp.exp2(s_scr[rows64(i), :].reshape(4, 16, ROWS) * SCALE2 - level16[None])
        p2[rows64(i), :] = p.reshape(64, ROWS).astype(BF16)
        return total + jnp.sum(p, axis=0)

    total = lax.fori_loop(0, NXY, soft2, jnp.zeros((16, ROWS), F32))
    l2 = [jnp.sum(total[0:8], axis=0, keepdims=True), jnp.sum(total[8:16], axis=0, keepdims=True)]
    o2 = nn(vblk_t[...], p2[...])
    w1, w2 = [], []
    squares = jnp.zeros((1, ROWS), F32)
    for h in range(2):
        cols = slice(h * DH, (h + 1) * DH)
        level = jnp.maximum(m1[h], m2[h])
        a1, a2 = jnp.exp2(m1[h] - level), jnp.exp2(m2[h] - level)
        inverse = 1.0 / (l1[h] * a1 + l2[h] * a2)
        w1.append(a1 * inverse)
        w2.append(a2 * inverse)
        out = (o1[cols, :] * w1[h] + o2[cols, :] * w2[h]).astype(BF16)
        att_t[cols, :] = out
        wide = out.astype(F32)
        squares = squares + jnp.sum(wide * wide, axis=0, keepdims=True)
    att[...] = att_t[...].T

    ahead_copy = remote(att.at[pl.ds(0, OFFMAX), :], ahead.at[pl.ds(0, OFFMAX), :], near_sem, 0, prv, sub)
    ahead_copy.start()
    s_scr[0:ROWS, :] = nn(att[...], att_t[...])

    def pick(i, carry):
        rows = rows64(i)
        here = idx[rows, :]
        low, high = here & 127, lax.shift_right_logical(here, 7)
        found = jnp.zeros((64, 128), F32)
        for b in range(4):
            value = pick_lanes(s_scr[rows, b * 128 : (b + 1) * 128], low)
            found = jnp.where(high == b, value, found)
        picked[rows, :] = found
        return carry

    lax.fori_loop(0, 8, pick, 0)
    ahead_copy.wait()
    late = slice(ROWS - 128, ROWS)
    far = nt(att[late, :], ahead[...])
    here = idx[late, :]
    picked[late, :] += jnp.where(lax.shift_right_logical(here, 7) == 4, pick_lanes(far, here & 127), 0.0)
    gram_ahead = nt(ahead[...], ahead[...])
    ahead_squares = jnp.sum(
        jnp.where(iota((128, 128), 0) == iota((128, 128), 1), gram_ahead, 0.0), axis=0, keepdims=True
    )

    pk_row = pl.multiple_of(sub * 16, 16)
    sq_row = pl.multiple_of(sub * 8, 8)
    for b in range(4):
        lanes = slice(b * 128, (b + 1) * 128)
        pk_buf[pl.ds(pk_row, 16), lanes] = picked[lanes, :].T[0:16, :].astype(BF16)
    sq_buf[pl.ds(sq_row, 8), :] = jnp.concatenate(
        [squares[:, b * 128 : (b + 1) * 128] for b in range(4)] + [ahead_squares, jnp.zeros((3, 128), F32)], axis=0
    )

    def sq_copy(j):
        part = sq_buf.at[pl.ds(sq_row, 8), :]
        return remote(part, part, sq_sem, j, seq, sub_peer(j))

    def pk_copy(j):
        part = pk_buf.at[pl.ds(pk_row, 16), :]
        return remote(part, part, pk_sem, j, seq, sub_peer(j))

    each(NSUB, sq_copy, start)
    each(NSUB, pk_copy, start)
    each(NSUB, sq_copy, finish)
    radius = jnp.sqrt(jnp.sum(sq_buf[...].reshape(NSUB, 8, 128), axis=0) / D + EPSILON)
    own_radius = jnp.concatenate([radius[b : b + 1, :] for b in range(4)], axis=1)
    parts = []
    for c in range(4):
        here = idx_t[:, c * 128 : (c + 1) * 128]
        low, high = here & 127, lax.shift_right_logical(here, 7)
        found = jnp.ones((16, 128), F32)
        for b in range(5 if c == 3 else 4):
            value = pick_lanes(jnp.broadcast_to(radius[b : b + 1, :], (16, 128)), low)
            found = jnp.where(high == b, value, found)
        parts.append(found)
    pair_radius = jnp.concatenate(parts, axis=1)
    factor = 1.0 / (D * TEMPER * own_radius * pair_radius)
    each(NSUB, pk_copy, finish)
    dots = jnp.sum(pk_buf[...].astype(F32).reshape(NSUB, 16, ROWS), axis=0)

    logits = dots * factor
    powers = jnp.exp(logits)
    expsum = jnp.sum(powers, axis=0, keepdims=True)
    step = (seq * ROWS + iota((1, ROWS), 1)).astype(F32)
    weight = (1.0 + 2.0 * step / TOKENS) / TOKENS
    first = (iota((16, ROWS), 0) == 15).astype(F32)
    loss_part = jnp.sum(weight * (jnp.log(expsum) - logits[15:16, :]), axis=1, keepdims=True)
    dlogits = (powers / expsum - first) * weight
    coef[...] = dlogits * factor
    pull = dlogits * logits
    rcoef[...] = pull / (D * pair_radius * pair_radius)
    own_pull = jnp.sum(pull, axis=0, keepdims=True) / (D * own_radius * own_radius)

    lxy_row = pl.multiple_of(xy * 8, 8)
    lz_row = pl.multiple_of(z * 8, 8)
    loss_xy[pl.ds(lxy_row, 8), :] = jnp.broadcast_to(loss_part, (8, 128))

    def lxy_copy(j):
        part = loss_xy.at[pl.ds(lxy_row, 8), :]
        return remote(part, part, lxy_sem, j, xy_peer(j), sub)

    def lz_copy(j):
        part = loss_z.at[pl.ds(lz_row, 8), :]
        return remote(part, part, lz_sem, j, z_peer(j), sub)

    each(NXY, lxy_copy, start)

    late_mark = iota((128, 128), 0) + ROWS == idx_t[15:16, late]
    far_c = jnp.where(late_mark, coef[15:16, late], 0.0)
    far_r = jnp.sum(jnp.where(late_mark, rcoef[15:16, late], 0.0), axis=1, keepdims=True)
    far_hi, far_lo = split(far_c)
    tail = nn(far_hi, att[late, :]) + nn(far_lo, att[late, :]) - far_r * ahead[...].astype(F32)
    tail_out[...] = tail.astype(BF16)
    tail_copy = remote(tail_out.at[pl.ds(0, OFFMAX), :], tail_in.at[pl.ds(0, OFFMAX), :], near_sem, 1, nxt, sub)
    tail_copy.start()

    row_c = iota((16, ROWS), 0)

    def table(i, carry):
        rows = pl.ds(pl.multiple_of(i * 16, 16), 16)
        here = row_c + i * 16
        pairs = jnp.zeros((16, ROWS), F32)
        pulls = jnp.zeros((16, ROWS), F32)
        for k in range(16):
            same = here == idx_t[k : k + 1, :]
            pairs = pairs + jnp.where(same, coef[k : k + 1, :], 0.0)
            pulls = pulls + jnp.where(same, rcoef[k : k + 1, :], 0.0)
        ct_hi[rows, :], ct_lo[rows, :] = split(pairs)
        h_hi[rows, :], h_lo[rows, :] = split(pulls)
        return carry

    lax.fori_loop(0, ROWS // 16, table, 0)
    ones = jnp.ones((16, ROWS), BF16)
    radial = nt(ones, h_hi[...])[0:1, :] + nt(ones, h_lo[...])[0:1, :] + own_pull
    mine = att_t[...]
    grad_t[...] = (
        nn(mine, ct_hi[...]) + nn(mine, ct_lo[...]) + nt(mine, ct_hi[...]) + nt(mine, ct_lo[...])
        - radial * mine.astype(F32)
    )
    grad_t[:, late] += tn(ahead[...], far_hi) + tn(ahead[...], far_lo)

    each(NXY, lxy_copy, finish)
    loss_z[pl.ds(lz_row, 8), :] = jnp.sum(loss_xy[...].reshape(NXY, 8, 128), axis=0)
    each(NZ, lz_copy, start)

    tail_copy.wait()
    grad_t[:, 0:128] += tail_in[...].astype(F32).T

    g1, g2, d1, d2 = [], [], [], []
    for h in range(2):
        cols = slice(h * DH, (h + 1) * DH)
        grad = grad_t[cols, :]
        wide = att_t[cols, :].astype(F32)
        one, two = (grad * w1[h]).astype(BF16), (grad * w2[h]).astype(BF16)
        g1.append(one)
        g2.append(two)
        d1.append(jnp.sum(one.astype(F32) * wide, axis=0, keepdims=True))
        d2.append(jnp.sum(two.astype(F32) * wide, axis=0, keepdims=True))
    both2 = jnp.concatenate(g2, axis=0)
    d16 = jnp.concatenate([jnp.broadcast_to(d2[0], (8, ROWS)), jnp.broadcast_to(d2[1], (8, ROWS))], axis=0)
    s_scr[...] = nn(vblk[...], both2)

    ds2 = kblk
    del ds2

    def slope2(i, carry):
        x = s_scr[rows64(i), :].reshape(4, 16, ROWS) - d16[None]
        p = p2[rows64(i), :].astype(F32).reshape(4, 16, ROWS)
        s_scr[rows64(i), :] = (x * p).reshape(64, ROWS)
        return carry

    lax.fori_loop(0, NXY, slope2, 0)
    slopes = s_scr[...].astype(BF16)
    in_first = (iota((PANEL, DH), 0) & 15) < 8
    key2 = nn(slopes, q_ref[...])
    gm[:, 0:DH] = (jnp.where(in_first, key2[:, :DH], key2[:, DH:]) * SCALE).astype(BF16)
    value2 = nt(p2[...], both2)
    gm[:, DH:FEAT] = jnp.where(in_first, value2[:, :DH], value2[:, DH:]).astype(BF16)

    def rs_copy(j):
        to = lax.rem(xy + j, NXY)
        return remote(
            gm.at[pl.ds(pl.multiple_of(to * 64, 64), 64), :], rs.at[pl.ds(block_row, 64), :],
            rs_sem, j, xy_peer(j), sub,
        )

    each(NXY, rs_copy, start)
    rs[pl.ds(block_row, 64), :] = gm[pl.ds(block_row, 64), :]
    query2 = nn(kblk_t[...], slopes)

    for h in range(2):
        cols = slice(h * DH, (h + 1) * DH)
        base = h * ROWS
        s_scr[base : base + ROWS, :] = nn(v_ref[:, cols], g1[h])

        def slope(i, carry, base=base, shift=d1[h]):
            x = s_scr[rows64(i, base), :] - shift
            s_scr[rows64(i, base), :] = x * p1[rows64(i, base), :].astype(F32)
            return carry

        lax.fori_loop(0, 8, slope, 0)
        near = s_scr[base : base + ROWS, :].astype(BF16)
        query = (nn(k_t[cols, :], near) + query2[cols, :]) * SCALE
        dq_ref[:, cols] = query.T.astype(BF16)
        dk_acc[:, cols] = nn(near, q_ref[:, cols]) * SCALE
        dv_acc[:, cols] = nt(p1[base : base + ROWS, :], g1[h])
    dk_ref[...] = dk_acc[...].astype(BF16)
    dv_ref[...] = dv_acc[...].astype(BF16)

    each(NZ, lz_copy, finish)
    loss_ref[...] = jnp.sum(loss_z[...].reshape(NZ, 8, 128), axis=0)
    each(NXY, rs_copy, finish)
    rz_out[...] = jnp.sum(rs[...].astype(F32).reshape(NXY, 64, FEAT), axis=0).astype(BF16)
    rz_row = pl.multiple_of(z * 16, 16)

    def rz_copy(j):
        to = lax.rem(z + j, NZ)
        return remote(
            rz_out.at[pl.ds(pl.multiple_of(to * 16, 16), 16), :], rz.at[pl.ds(rz_row, 16), :],
            rz_sem, j, z_peer(j), sub,
        )

    each(NZ, rz_copy, start)
    rz[pl.ds(rz_row, 16), :] = rz_out[pl.ds(rz_row, 16), :]
    each(NZ, rz_copy, finish)
    term = jnp.sum(rz[...].astype(F32).reshape(NZ, 16, FEAT), axis=0)
    last = iota((16, FEAT), 0) == 15
    for i in range(8):
        rows = slice(i * STRIDE + STRIDE - 16, (i + 1) * STRIDE)
        for acc, ref, lanes in ((dk_acc, dk_ref, slice(0, DH)), (dv_acc, dv_ref, slice(DH, FEAT))):
            extra = jnp.concatenate([term[i : i + 1, lanes], term[8 + i : 9 + i, lanes]], axis=1)
            ref[rows, :] = (acc[rows, :] + jnp.where(last, extra, 0.0)).astype(BF16)


def local(queries, keys, values, offsets, negatives):
    vmem = pl.BlockSpec(memory_space=pltpu.VMEM)
    wide = jax.ShapeDtypeStruct((ROWS, FEAT), BF16)

    def sems(count):
        return pltpu.SemaphoreType.DMA((2, count))

    outs = pl.pallas_call(
        kernel,
        out_shape=(wide, wide, wide, jax.ShapeDtypeStruct((8, 128), F32)),
        in_specs=[vmem] * 5,
        out_specs=(vmem,) * 4,
        scratch_shapes=[
            pltpu.VMEM((PANEL, FEAT), BF16),
            pltpu.VMEM((PANEL, FEAT), BF16),
            pltpu.VMEM((PANEL, FEAT), BF16),
            pltpu.VMEM((FEAT, PANEL), BF16),
            pltpu.VMEM((FEAT, PANEL), BF16),
            pltpu.VMEM((FEAT, ROWS), BF16),
            pltpu.VMEM((FEAT, ROWS), BF16),
            pltpu.VMEM((PANEL, ROWS), F32),
            pltpu.VMEM((PANEL, ROWS), BF16),
            pltpu.VMEM((PANEL, ROWS), BF16),
            pltpu.VMEM((FEAT, ROWS), F32),
            pltpu.VMEM((ROWS, FEAT), BF16),
            pltpu.VMEM((FEAT, ROWS), BF16),
            pltpu.VMEM((128, FEAT), BF16),
            pltpu.VMEM((ROWS, 128), I32),
            pltpu.VMEM((16, ROWS), I32),
            pltpu.VMEM((ROWS, 128), F32),
            pltpu.VMEM((NSUB * 16, ROWS), BF16),
            pltpu.VMEM((NSUB * 8, 128), F32),
            pltpu.VMEM((16, ROWS), F32),
            pltpu.VMEM((16, ROWS), F32),
            pltpu.VMEM((ROWS, ROWS), BF16),
            pltpu.VMEM((ROWS, ROWS), BF16),
            pltpu.VMEM((ROWS, ROWS), BF16),
            pltpu.VMEM((ROWS, ROWS), BF16),
            pltpu.VMEM((FEAT, ROWS), F32),
            pltpu.VMEM((128, FEAT), BF16),
            pltpu.VMEM((128, FEAT), BF16),
            pltpu.VMEM((NXY * 8, 128), F32),
            pltpu.VMEM((NZ * 8, 128), F32),
            pltpu.VMEM((PANEL, FEAT), BF16),
            pltpu.VMEM((PANEL, FEAT), BF16),
            pltpu.VMEM((64, FEAT), BF16),
            pltpu.VMEM((64, FEAT), BF16),
            pltpu.VMEM((ROWS, FEAT), F32),
            pltpu.VMEM((ROWS, FEAT), F32),
            sems(NZ), sems(NXY), sems(2), sems(NSUB), sems(NSUB), sems(NXY), sems(NZ), sems(NXY), sems(NZ),
        ],
        compiler_params=pltpu.CompilerParams(
            collective_id=0, has_side_effects=True, vmem_limit_bytes=48 * 1024 * 1024
        ),
    )(queries, keys, values, offsets.reshape(4, 128), negatives)
    return outs[0], outs[1], outs[2], outs[3][0, 0]


def solution(mesh):
    placed = (P("seq", "sub"), P("seq", "sub"), P("seq", "sub"), P("seq"), P("seq", None))
    return jax.shard_map(
        local,
        mesh=mesh,
        in_specs=placed,
        out_specs=(P("seq", "sub"), P("seq", "sub"), P("seq", "sub"), P()),
        check_vma=False,
    )
```

time: 1180 us -> 77.4 us (0.07)
  the two profiles are of different devices: /device:TPU:32 before, /device:TPU:28 now
where the time goes in v1:
time: 77.4 us; the launch traced here: 77.2 us
  Pallas kernels  71 us (92%)
  local copies, waits for them, and re-layouts  5.46 us (7%)
    pallas_call x1, Pallas kernels, local(): pl.pallas_call(kernel, out_shape=(wide, wide, wide, jax.ShapeDtypeStruct(...  71 us
    unnamed x12, local copies, waits for them, and re-layouts  4.95 us

profile of v1, /device:TPU:28, one launch (start us, length us, event | category | flops | bytes accessed | tf_op | source)
XLA Modules:
  0.0 77.2 jit_solution(11829876068971953450)
XLA Ops:
  0.6 0.0 copy-start
  0.6 0.0 copy-start.3
  0.7 0.9 %copy.9.neg_ref = s32[512,15]{1,0:T(8,128)S(1)} copy(s32[512,15]{0,1:T(8,128)} %param.9) | data formatting | bytes 61440 | tf_op args[4]
  1.6 0.0 copy-done
  1.6 0.0 copy-done.3
  1.6 0.0 copy-start.1
  1.6 0.9 %copy-done.1 = bf16[512,256]{1,0:T(8,128)(2,1)S(1)} copy-done((bf16[512,256]{1,0:T(8,128)(2,1)S(1)}, bf16[512,256]{1,0:T(8,128)(2,1)}, u32[]{:S(2)}) %copy-start.1) | copy-done | bytes 262168
  2.6 0.0 copy-start.2
  2.6 0.9 %copy-done.2 = bf16[512,256]{1,0:T(8,128)(2,1)S(1)} copy-done((bf16[512,256]{1,0:T(8,128)(2,1)S(1)}, bf16[512,256]{1,0:T(8,128)(2,1)}, u32[]{:S(2)}) %copy-start.2) | copy-done | bytes 262168
  3.5 71.0 %shard_map.84 = (bf16[512,256]{1,0:T(8,128)(2,1)S(1)}, bf16[512,256]{1,0:T(8,128)(2,1)S(1)}, bf16[512,256]{1,0:T(8,128)(2,1)S(1)}, f32[8,128]{1,0:T(8,128)S(1)}) custom-call(bf16[512,256]{1,0:T(8,128)(2,1)S(1)} %copy-done, bf16[512,256]{1,0:T(8,128)(2,1)S(1)} %copy-done.1, bf16[512,256]{1,0:T(8,128)(2,1)S(1)} %copy-done.2, s32[4,128]{1,0:T(4,128)S(1)} %bitcast.2, ...), custom_call_target="tpu_custom_call" | custom-call | tf_op jit(solution)/shard_map/pallas_call | solution.py:462
  74.5 0.5 slice.3
  75.0 0.7 copy.13
  75.8 0.7 copy.14
  76.5 0.7 copy.15
Async XLA Ops:
  0.6 1.0 %copy-start = (bf16[512,256]{1,0:T(8,128)(2,1)S(1)}, bf16[512,256]{1,0:T(8,128)(2,1)}, u32[]{:S(2)}) copy-start(bf16[512,256]{1,0:T(8,128)(2,1)} %q_ref.1) | copy-start | bytes 786436
  0.6 1.0 %copy-start.3 = (s32[512]{0:T(512)S(1)}, s32[512]{0:T(512)}, u32[]{:S(2)}) copy-start(s32[512]{0:T(512)} %param.8) | copy-start | bytes 6148
  1.6 1.0 %copy-start.1 = (bf16[512,256]{1,0:T(8,128)(2,1)S(1)}, bf16[512,256]{1,0:T(8,128)(2,1)}, u32[]{:S(2)}) copy-start(bf16[512,256]{1,0:T(8,128)(2,1)} %k_ref.1) | copy-start | bytes 786436
  2.6 0.9 %copy-start.2 = (bf16[512,256]{1,0:T(8,128)(2,1)S(1)}, bf16[512,256]{1,0:T(8,128)(2,1)}, u32[]{:S(2)}) copy-start(bf16[512,256]{1,0:T(8,128)(2,1)} %v_ref.1) | copy-start | bytes 786436

commit v2 on v1

v2 whole, which is shorter than its diff:
```python
import math

import jax
import jax.numpy as jnp
from jax import lax
from jax.experimental import pallas as pl
from jax.experimental.pallas import tpu as pltpu
from jax.sharding import PartitionSpec as P

DH = 128
D = 2048
ROWS = 512
FEAT = 256
STRIDE = 64
OFFMAX = 64
NZ = 4
NXY = 16
NSUB = 8
NSEQ = 64
TOKENS = 32768
PANEL = 1024
WIDE = 640

EPSILON = 1e-05
TEMPER = 0.1
MASKED = -1e30
SCALE = 1.0 / math.sqrt(DH)
SCALE2 = SCALE * math.log2(math.e)

F32 = jnp.float32
BF16 = jnp.bfloat16
I32 = jnp.int32
MESH = pl.DeviceIdType.MESH


def nn(a, b):
    return lax.dot_general(a, b, (((1,), (0,)), ((), ())), preferred_element_type=F32)


def nt(a, b):
    return lax.dot_general(a, b, (((1,), (1,)), ((), ())), preferred_element_type=F32)


def tn(a, b):
    return lax.dot_general(a, b, (((0,), (0,)), ((), ())), preferred_element_type=F32)


def iota(shape, dim):
    return lax.broadcasted_iota(I32, shape, dim)


def pick_lanes(x, index):
    return jnp.take_along_axis(x, index, axis=1, mode="promise_in_bounds")


def split(x):
    high = x.astype(BF16)
    return high, (x - high.astype(F32)).astype(BF16)


def kernel(
    q_hbm, k_hbm, v_hbm, off_hbm, neg_hbm,
    dq_ref, dk_ref, dv_ref, loss_ref,
    q, k, v, off, neg, kx, vx, gat, kblk, vblk, kblk_t, vblk_t, k_t, v_t, s_scr, p1, p2, o1, att, att_t,
    idx, idx_t, picked, pk_buf, sq_buf, coef, rcoef, ct_hi, ct_lo, radial, grad_t,
    tail_out, tail_in, loss_xy, loss_z, ds2, query2, gm, rs, rz_out, rz, own_term, dk_acc, dv_acc,
    load_sem, z_sem, own_sem, low_sem, mid_sem, near_sem, pk_sem, sq_sem, lxy_sem, lz_sem, rs_sem, rz_sem,
):
    seq = lax.axis_index("seq").astype(I32)
    sub = lax.axis_index("sub").astype(I32)
    z, xy = lax.div(seq, NXY), lax.rem(seq, NXY)
    nxt, prv = lax.rem(seq + 1, NSEQ), lax.rem(seq + NSEQ - 1, NSEQ)

    def z_seq(to):
        return to * NXY + xy

    def xy_peer(j):
        return z * NXY + lax.rem(xy + j, NXY)

    def sub_peer(j):
        return lax.rem(sub + j, NSUB)

    def remote(src, dst, sems, j, to_seq, to_sub):
        return pltpu.make_async_remote_copy(
            src_ref=src, dst_ref=dst, send_sem=sems.at[0, j], recv_sem=sems.at[1, j],
            device_id=(to_seq, to_sub), device_id_type=MESH,
        )

    def each(count, make, act):
        def body(j, carry):
            act(make(j))
            return carry

        lax.fori_loop(1, count, body, 0)

    def start(copy):
        copy.start()

    def finish(copy):
        copy.wait()

    loads = [
        pltpu.make_async_copy(src, dst, load_sem.at[i])
        for i, (src, dst) in enumerate(
            [(k_hbm, k), (v_hbm, v), (q_hbm, q.at[pl.ds(0, ROWS), :]), (off_hbm, off), (neg_hbm, neg)]
        )
    ]
    for load in loads:
        load.start()

    gat[...] = jnp.zeros((NZ, NXY * 16, FEAT), BF16)
    rz[...] = jnp.zeros((NZ * 16, FEAT), BF16)
    tail_in[...] = jnp.zeros((128, FEAT), BF16)
    barrier = pltpu.get_barrier_semaphore()

    def greet(to_seq, to_sub):
        pl.semaphore_signal(barrier, inc=1, device_id=(to_seq, to_sub), device_id_type=MESH)

    greet(z_seq(lax.rem(z + 1, NZ)), sub)
    greet(z_seq(lax.rem(z + 3, NZ)), sub)

    @pl.when(z < 2)
    def _():
        greet(z_seq(z + 2), sub)

    each(NXY, xy_peer, lambda to: greet(to, sub))
    greet(nxt, sub)
    greet(prv, sub)
    each(NSUB, sub_peer, lambda to: greet(seq, to))

    own_row = pl.multiple_of(xy * 16, 16)
    own_rows = pl.ds(own_row, 16)
    chosen = (iota((16, ROWS), 1) == (iota((16, ROWS), 0) & 7) * STRIDE + (STRIDE - 1)).astype(F32).astype(BF16)
    first8 = iota((16, DH), 0) < 8
    loads[0].wait()
    loads[1].wait()
    k_sel = nn(chosen, k[...])
    v_sel = nn(chosen, v[...])
    gat[z, own_rows, :] = jnp.concatenate(
        [
            jnp.where(first8, k_sel[:, :DH], k_sel[:, DH:]),
            jnp.where(first8, v_sel[:, :DH], v_sel[:, DH:]),
        ],
        axis=1,
    ).astype(BF16)
    loads[2].wait()
    q[ROWS + OFFMAX :, :] = jnp.zeros((WIDE - ROWS - OFFMAX, FEAT), BF16)

    pl.semaphore_wait(barrier, 2 + (NXY - 1) + 2 + (NSUB - 1) + lax.div(z, 2))

    pair = gat.at[pl.ds(0, 2), own_rows, :]
    mine_tile = gat.at[z, own_rows, :]

    def swap():
        return remote(mine_tile, mine_tile, z_sem, 0, z_seq(1 - z), sub)

    def relay(to):
        return remote(pair, pair, z_sem, 1, z_seq(to), sub)

    def third():
        tile = gat.at[2, own_rows, :]
        return remote(tile, tile, z_sem, 2, z_seq(3), sub)

    def own_copy(j):
        return remote(mine_tile, mine_tile, own_sem, j, xy_peer(j), sub)

    def low_copy(count):
        part = gat.at[pl.ds(0, count), own_rows, :]
        return lambda j: remote(part, part, low_sem, j, xy_peer(j), sub)

    def mid_copy(j):
        part = gat.at[2, own_rows, :]
        return remote(part, part, mid_sem, j, xy_peer(j), sub)

    @pl.when(z < 2)
    def _():
        swap().start()

    @pl.when(z == 2)
    def _():
        third().start()

    each(NXY, own_copy, start)
    near = [
        remote(q.at[pl.ds(0, OFFMAX), :], q.at[pl.ds(ROWS, OFFMAX), :], near_sem, 0, prv, sub),
        remote(k.at[pl.ds(0, OFFMAX), :], kx, near_sem, 1, prv, sub),
        remote(v.at[pl.ds(0, OFFMAX), :], vx, near_sem, 2, prv, sub),
    ]
    for copy in near:
        copy.start()

    @pl.when(z == 0)
    def _():
        swap().wait()
        relay(3).start()

    @pl.when(z == 1)
    def _():
        swap().wait()
        relay(2).start()
        each(NXY, low_copy(1), start)

    @pl.when(z == 2)
    def _():
        relay(2).wait_recv()
        each(NXY, low_copy(2), start)

    @pl.when(z == 3)
    def _():
        third().wait_recv()
        each(NXY, mid_copy, start)
        relay(3).wait_recv()
        each(NXY, low_copy(2), start)

    loads[3].wait()
    loads[4].wait()
    k_t[...] = k[...].T
    v_t[...] = v[...].T
    idx_t[0:15, :] = neg[...]
    for b in range(4):
        cols = slice(b * 128, (b + 1) * 128)
        idx_t[15:16, cols] = off[b : b + 1, :] + iota((1, 128), 1) + b * 128
    for b in range(4):
        cols = slice(b * 128, (b + 1) * 128)
        idx[cols, :] = jnp.concatenate([idx_t[:, cols], jnp.zeros((112, 128), I32)], axis=0).T

    lane_q = iota((64, ROWS), 1)
    row_k = iota((64, ROWS), 0)

    def rows64(i, base=0):
        return pl.ds(pl.multiple_of(base + i * 64, 64), 64)

    m1, l1 = [], []
    for h in range(2):
        cols = slice(h * DH, (h + 1) * DH)
        base = h * ROWS
        s_scr[base : base + ROWS, 0:ROWS] = nt(k[:, cols], q[0:ROWS, cols])

        def top(i, best, base=base):
            x = s_scr[rows64(i, base), 0:ROWS]
            x = jnp.where(row_k + i * 64 <= lane_q, x, MASKED)
            s_scr[rows64(i, base), 0:ROWS] = x
            return jnp.maximum(best, jnp.max(x.reshape(8, 8, ROWS), axis=0))

        best = lax.fori_loop(0, 8, top, jnp.full((8, ROWS), MASKED, F32))
        level = jnp.max(best, axis=0, keepdims=True) * SCALE2

        def soft(i, total, base=base, level=level):
            p = jnp.exp2(s_scr[rows64(i, base), 0:ROWS] * SCALE2 - level)
            p1[rows64(i, base), :] = p.astype(BF16)
            return total + jnp.sum(p.reshape(8, 8, ROWS), axis=0)

        total = lax.fori_loop(0, 8, soft, jnp.zeros((8, ROWS), F32))
        m1.append(level)
        l1.append(jnp.sum(total, axis=0, keepdims=True))
        o1[cols, 0:ROWS] = nn(v_t[cols, :], p1[base : base + ROWS, :])
    for copy in near:
        copy.wait()
    for h in range(2):
        cols = slice(h * DH, (h + 1) * DH)
        x = nt(kx[:, cols], q[ROWS:WIDE, cols])
        x = jnp.where(iota((64, 128), 0) <= iota((64, 128), 1), x, MASKED)
        level = jnp.max(x, axis=0, keepdims=True) * SCALE2
        p = jnp.exp2(x * SCALE2 - level)
        m1[h] = jnp.concatenate([m1[h], level], axis=1)
        l1[h] = jnp.concatenate([l1[h], jnp.sum(p, axis=0, keepdims=True)], axis=1)
        o1[cols, ROWS:WIDE] = tn(vx[:, cols], p.astype(BF16))

    each(NXY, own_copy, finish)

    @pl.when(z == 1)
    def _():
        each(NXY, low_copy(1), finish)

    @pl.when(z == 2)
    def _():
        each(NXY, low_copy(2), finish)

    @pl.when(z == 3)
    def _():
        each(NXY, mid_copy, finish)
        each(NXY, low_copy(2), finish)

    in_first = (iota((256, DH), 0) & 15) < 8
    one = jnp.where(in_first, 1.0, 0.0).astype(BF16)
    two = jnp.where(in_first, 0.0, 1.0).astype(BF16)
    in_first_t = (iota((DH, 256), 1) & 15) < 8
    one_t = jnp.where(in_first_t, 1.0, 0.0).astype(BF16)
    two_t = jnp.where(in_first_t, 0.0, 1.0).astype(BF16)
    for b in range(NZ):
        rows = slice(b * 256, (b + 1) * 256)
        for lanes, blk, blk_t in ((slice(0, DH), kblk, kblk_t), (slice(DH, FEAT), vblk, vblk_t)):
            tile = gat[b, :, lanes]
            tile_t = tile.T
            blk[rows, 0:DH] = tile * one
            blk[rows, DH:FEAT] = tile * two
            blk_t[0:DH, rows] = tile_t * one_t
            blk_t[DH:FEAT, rows] = tile_t * two_t

    s_scr[...] = nt(kblk[...], q[...])
    slab = lax.shift_right_logical(iota((64, WIDE), 0), 4)
    limit = jnp.where(iota((1, WIDE), 1) < ROWS, seq, nxt)

    def top2(i, best):
        x = s_scr[rows64(i), :]
        x = jnp.where(slab + i * 4 < limit, x, MASKED)
        s_scr[rows64(i), :] = x
        return jnp.maximum(best, jnp.max(x.reshape(4, 16, WIDE), axis=0))

    best = lax.fori_loop(0, NXY, top2, jnp.full((16, WIDE), MASKED, F32))
    m2 = [jnp.max(best[0:8], axis=0, keepdims=True) * SCALE2, jnp.max(best[8:16], axis=0, keepdims=True) * SCALE2]
    level16 = jnp.concatenate([jnp.broadcast_to(m2[0], (8, WIDE)), jnp.broadcast_to(m2[1], (8, WIDE))], axis=0)

    def soft2(i, total):
        p = jnp.exp2(s_scr[rows64(i), :].reshape(4, 16, WIDE) * SCALE2 - level16[None])
        p2[rows64(i), :] = p.reshape(64, WIDE).astype(BF16)
        return total + jnp.sum(p, axis=0)

    total = lax.fori_loop(0, NXY, soft2, jnp.zeros((16, WIDE), F32))
    l2 = [jnp.sum(total[0:8], axis=0, keepdims=True), jnp.sum(total[8:16], axis=0, keepdims=True)]
    o2 = nn(vblk_t[...], p2[...])
    w1, w2 = [], []
    squares = jnp.zeros((1, WIDE), F32)
    for h in range(2):
        cols = slice(h * DH, (h + 1) * DH)
        level = jnp.maximum(m1[h], m2[h])
        a1, a2 = jnp.exp2(m1[h] - level), jnp.exp2(m2[h] - level)
        inverse = 1.0 / (l1[h] * a1 + l2[h] * a2)
        a1, a2 = a1 * inverse, a2 * inverse
        w1.append(a1[:, 0:ROWS])
        w2.append(a2[:, 0:ROWS])
        out = (o1[cols, :] * a1 + o2[cols, :] * a2).astype(BF16)
        att_t[cols, :] = out
        wide = out.astype(F32)
        squares = squares + jnp.sum(wide * wide, axis=0, keepdims=True)

    sq_row = pl.multiple_of(sub * 8, 8)
    sq_buf[pl.ds(sq_row, 8), :] = jnp.concatenate(
        [squares[:, b * 128 : (b + 1) * 128] for b in range(5)] + [jnp.zeros((3, 128), F32)], axis=0
    )

    def sq_copy(j):
        part = sq_buf.at[pl.ds(sq_row, 8), :]
        return remote(part, part, sq_sem, j, seq, sub_peer(j))

    each(NSUB, sq_copy, start)
    att[...] = att_t[...].T
    s_scr[0:ROWS, :] = nn(att[0:ROWS, :], att_t[...])

    def pick(i, carry):
        rows = rows64(i)
        here = idx[rows, :]
        low, high = here & 127, lax.shift_right_logical(here, 7)
        found = jnp.zeros((64, 128), F32)
        for b in range(5):
            value = pick_lanes(s_scr[rows, b * 128 : (b + 1) * 128], low)
            found = jnp.where(high == b, value, found)
        picked[rows, :] = found
        return carry

    lax.fori_loop(0, 8, pick, 0)
    pk_row = pl.multiple_of(sub * 16, 16)
    for b in range(4):
        lanes = slice(b * 128, (b + 1) * 128)
        pk_buf[pl.ds(pk_row, 16), lanes] = picked[lanes, :].T[0:16, :].astype(BF16)

    def pk_copy(j):
        part = pk_buf.at[pl.ds(pk_row, 16), :]
        return remote(part, part, pk_sem, j, seq, sub_peer(j))

    each(NSUB, pk_copy, start)
    each(NSUB, sq_copy, finish)
    radius = jnp.sqrt(jnp.sum(sq_buf[...].reshape(NSUB, 8, 128), axis=0) / D + EPSILON)
    own_radius = jnp.concatenate([radius[b : b + 1, :] for b in range(4)], axis=1)
    parts = []
    for c in range(4):
        here = idx_t[:, c * 128 : (c + 1) * 128]
        low, high = here & 127, lax.shift_right_logical(here, 7)
        found = jnp.ones((16, 128), F32)
        for b in range(5 if c == 3 else 4):
            value = pick_lanes(jnp.broadcast_to(radius[b : b + 1, :], (16, 128)), low)
            found = jnp.where(high == b, value, found)
        parts.append(found)
    pair_radius = jnp.concatenate(parts, axis=1)
    factor = 1.0 / (D * TEMPER * own_radius * pair_radius)
    pair_share = 1.0 / (D * pair_radius * pair_radius)
    own_share = 1.0 / (D * own_radius * own_radius)
    each(NSUB, pk_copy, finish)
    dots = jnp.sum(pk_buf[...].astype(F32).reshape(NSUB, 16, ROWS), axis=0)

    logits = dots * factor
    powers = jnp.exp(logits)
    expsum = jnp.sum(powers, axis=0, keepdims=True)
    step = (seq * ROWS + iota((1, ROWS), 1)).astype(F32)
    weight = (1.0 + 2.0 * step / TOKENS) / TOKENS
    first = (iota((16, ROWS), 0) == 15).astype(F32)
    dlogits = (powers / expsum - first) * weight
    coef[...] = dlogits * factor
    pull = dlogits * logits
    rcoef[...] = pull * pair_share
    own_pull = jnp.sum(pull, axis=0, keepdims=True) * own_share

    late = slice(ROWS - 128, ROWS)
    ahead = att[ROWS:WIDE, :]
    late_mark = iota((128, 128), 0) + ROWS == idx_t[15:16, late]
    far_c = jnp.where(late_mark, coef[15:16, late], 0.0)
    far_r = jnp.sum(jnp.where(late_mark, rcoef[15:16, late], 0.0), axis=1, keepdims=True)
    far_hi, far_lo = split(far_c)
    tail = nn(far_hi, att[late, :]) + nn(far_lo, att[late, :]) - far_r * ahead.astype(F32)
    tail_out[...] = tail.astype(BF16)
    tail_copy = remote(tail_out.at[pl.ds(0, OFFMAX), :], tail_in.at[pl.ds(0, OFFMAX), :], near_sem, 3, nxt, sub)
    tail_copy.start()

    loss_part = jnp.sum(weight * (jnp.log(expsum) - logits[15:16, :]), axis=1, keepdims=True)
    lxy_row = pl.multiple_of(xy * 8, 8)
    loss_xy[pl.ds(lxy_row, 8), :] = jnp.broadcast_to(loss_part, (8, 128))

    def lxy_copy(j):
        part = loss_xy.at[pl.ds(lxy_row, 8), :]
        return remote(part, part, lxy_sem, j, xy_peer(j), sub)

    each(NXY, lxy_copy, start)
    row_c = iota((16, ROWS), 0)

    def table(i, carry):
        rows = pl.ds(pl.multiple_of(i * 16, 16), 16)
        here = row_c + i * 16
        pairs = jnp.zeros((16, ROWS), F32)
        pulls = jnp.zeros((16, ROWS), F32)
        for k in range(16):
            same = here == idx_t[k : k + 1, :]
            pairs = pairs + jnp.where(same, coef[k : k + 1, :], 0.0)
            pulls = pulls + jnp.where(same, rcoef[k : k + 1, :], 0.0)
        ct_hi[rows, :], ct_lo[rows, :] = split(pairs)
        radial[rows, :] = jnp.sum(pulls, axis=1, keepdims=True)
        return carry

    lax.fori_loop(0, ROWS // 16, table, 0)
    rows_own = att[0:ROWS, :]
    cols_own = att_t[:, 0:ROWS]
    pushed = nn(ct_hi[...], rows_own) + nn(ct_lo[...], rows_own) - radial[...] * rows_own.astype(F32)
    grad_t[...] = nn(cols_own, ct_hi[...]) + nn(cols_own, ct_lo[...]) - own_pull * cols_own.astype(F32) + pushed.T
    grad_t[:, late] += tn(ahead, far_hi) + tn(ahead, far_lo)
    tail_copy.wait()
    grad_t[:, 0:128] += tail_in[...].astype(F32).T

    g1, g2, d1, d2 = [], [], [], []
    for h in range(2):
        cols = slice(h * DH, (h + 1) * DH)
        grad = grad_t[cols, :]
        wide = att_t[cols, 0:ROWS].astype(F32)
        one, two = (grad * w1[h]).astype(BF16), (grad * w2[h]).astype(BF16)
        g1.append(one)
        g2.append(two)
        d1.append(jnp.sum(one.astype(F32) * wide, axis=0, keepdims=True))
        d2.append(jnp.sum(two.astype(F32) * wide, axis=0, keepdims=True))
    both2 = jnp.concatenate(g2, axis=0)
    d16 = jnp.concatenate([jnp.broadcast_to(d2[0], (8, ROWS)), jnp.broadcast_to(d2[1], (8, ROWS))], axis=0)

    def rows256(w):
        return pl.ds(pl.multiple_of(w * 256, 256), 256)

    def rs_copy(w):
        def make(j):
            to = pl.ds(pl.multiple_of(lax.rem(xy + j, NXY) * 16, 16), 16)
            return remote(gm.at[w, to, :], rs.at[w, own_rows, :], rs_sem, w * NXY + j, xy_peer(j), sub)

        return make

    def wave(w, carry):
        rows = rows256(w)
        s_scr[0:256, 0:ROWS] = nn(vblk[rows, :], both2)

        def slope(i, carry):
            x = s_scr[rows64(i), 0:ROWS].reshape(4, 16, ROWS) - d16[None]
            here = rows64(i, w * 256)
            p = p2[here, 0:ROWS].astype(F32).reshape(4, 16, ROWS)
            ds2[here, :] = (x * p).reshape(64, ROWS).astype(BF16)
            return carry

        lax.fori_loop(0, 4, slope, 0)
        head0 = (iota((256, DH), 0) & 15) < 8
        key2 = nn(ds2[rows, :], q[0:ROWS, :])
        value2 = nt(p2[rows, 0:ROWS], both2)
        gm[w, :, 0:DH] = (jnp.where(head0, key2[:, :DH], key2[:, DH:]) * SCALE).astype(BF16)
        gm[w, :, DH:FEAT] = jnp.where(head0, value2[:, :DH], value2[:, DH:]).astype(BF16)
        each(NXY, rs_copy(w), start)
        rs[w, own_rows, :] = gm[w, own_rows, :]
        return carry

    lax.fori_loop(0, z + 1, wave, 0)

    each(NXY, lxy_copy, finish)
    plane_loss = jnp.sum(loss_xy[...].reshape(NXY, 8, 128), axis=0)
    loss_z[0:8, :] = plane_loss
    lz_first = remote(loss_z.at[pl.ds(0, 8), :], loss_z.at[pl.ds(8, 8), :], lz_sem, 0, z_seq(z + 1 - 2 * lax.rem(z, 2)), sub)
    lz_first.start()

    query2[...] = jnp.zeros((FEAT, ROWS), F32)

    def far_query(w, carry):
        query2[...] += nn(kblk_t[:, rows256(w)], ds2[rows256(w), :])
        return carry

    lax.fori_loop(0, z + 1, far_query, 0)
    for h in range(2):
        cols = slice(h * DH, (h + 1) * DH)
        base = h * ROWS
        s_scr[base : base + ROWS, 0:ROWS] = nn(v[:, cols], g1[h])

        def slope1(i, carry, base=base, shift=d1[h]):
            x = s_scr[rows64(i, base), 0:ROWS] - shift
            s_scr[rows64(i, base), 0:ROWS] = x * p1[rows64(i, base), :].astype(F32)
            return carry

        lax.fori_loop(0, 8, slope1, 0)
        close = s_scr[base : base + ROWS, 0:ROWS].astype(BF16)
        query = (nn(k_t[cols, :], close) + query2[cols, :]) * SCALE
        dq_ref[:, cols] = query.T.astype(BF16)
        dk_acc[:, cols] = nn(close, q[0:ROWS, cols]) * SCALE
        dv_acc[:, cols] = nt(p1[base : base + ROWS, :], g1[h])
    dk_ref[...] = dk_acc[...].astype(BF16)
    dv_ref[...] = dv_acc[...].astype(BF16)

    def plane_sum(w):
        each(NXY, rs_copy(w), finish)
        return jnp.sum(rs[w].astype(F32).reshape(NXY, 16, FEAT), axis=0)

    rz_row = pl.multiple_of(z * 16, 16)

    def rz_copy(w):
        part = pl.ds(pl.multiple_of(w * 16, 16), 16)
        return remote(rz_out.at[part, :], rz.at[pl.ds(rz_row, 16), :], rz_sem, z - w, z_seq(w), sub)

    def down(w, carry):
        rz_out[pl.ds(pl.multiple_of(w * 16, 16), 16), :] = plane_sum(w).astype(BF16)
        rz_copy(w).start()
        return carry

    lax.fori_loop(0, z, down, 0)
    own_term[...] = plane_sum(z)
    lz_first.wait()
    loss_z[16:24, :] = loss_z[0:8, :] + loss_z[8:16, :]
    lz_second = remote(loss_z.at[pl.ds(16, 8), :], loss_z.at[pl.ds(24, 8), :], lz_sem, 1, z_seq(3 - z), sub)
    lz_second.start()

    def sent(w, carry):
        rz_copy(w).wait_send()
        return carry

    lax.fori_loop(0, z, sent, 0)

    def arrived(j, carry):
        slot = pl.ds(pl.multiple_of((z + j) * 16, 16), 16)
        remote(rz_out.at[pl.ds(0, 16), :], rz.at[slot, :], rz_sem, j, z_seq(z + j), sub).wait_recv()
        return carry

    lax.fori_loop(1, NZ - z, arrived, 0)
    term = own_term[...] + jnp.sum(rz[...].astype(F32).reshape(NZ, 16, FEAT), axis=0)
    last = iota((16, FEAT), 0) == 15
    for i in range(8):
        rows = slice(i * STRIDE + STRIDE - 16, (i + 1) * STRIDE)
        for acc, ref, lanes in ((dk_acc, dk_ref, slice(0, DH)), (dv_acc, dv_ref, slice(DH, FEAT))):
            extra = jnp.concatenate([term[i : i + 1, lanes], term[8 + i : 9 + i, lanes]], axis=1)
            ref[rows, :] = (acc[rows, :] + jnp.where(last, extra, 0.0)).astype(BF16)
    lz_second.wait()
    loss_ref[...] = loss_z[16:24, :] + loss_z[24:32, :]

    @pl.when(z < 2)
    def _():
        relay(3).wait_send()

    @pl.when(z == 2)
    def _():
        third().wait_send()


def emit(dq, dk, dv, loss, dq_out, dk_out, dv_out, loss_out, sems):
    copies = [
        pltpu.make_async_copy(src, dst, sems.at[i])
        for i, (src, dst) in enumerate([(dq, dq_out), (dk, dk_out), (dv, dv_out)])
    ]
    for copy in copies:
        copy.start()
    loss_out[...] = loss[0:1, 0:1]
    for copy in copies:
        copy.wait()


def local(queries, keys, values, offsets, negatives):
    vmem = pl.BlockSpec(memory_space=pltpu.VMEM)
    anywhere = pl.BlockSpec(memory_space=pl.ANY)
    wide = jax.ShapeDtypeStruct((ROWS, FEAT), BF16)

    def sems(count):
        return pltpu.SemaphoreType.DMA((2, count))

    outs = pl.pallas_call(
        kernel,
        out_shape=(wide, wide, wide, jax.ShapeDtypeStruct((8, 128), F32)),
        in_specs=[anywhere] * 5,
        out_specs=(vmem,) * 4,
        scratch_shapes=[
            pltpu.VMEM((WIDE, FEAT), BF16),
            pltpu.VMEM((ROWS, FEAT), BF16),
            pltpu.VMEM((ROWS, FEAT), BF16),
            pltpu.VMEM((4, 128), I32),
            pltpu.VMEM((15, ROWS), I32),
            pltpu.VMEM((OFFMAX, FEAT), BF16),
            pltpu.VMEM((OFFMAX, FEAT), BF16),
            pltpu.VMEM((NZ, NXY * 16, FEAT), BF16),
            pltpu.VMEM((PANEL, FEAT), BF16),
            pltpu.VMEM((PANEL, FEAT), BF16),
            pltpu.VMEM((FEAT, PANEL), BF16),
            pltpu.VMEM((FEAT, PANEL), BF16),
            pltpu.VMEM((FEAT, ROWS), BF16),
            pltpu.VMEM((FEAT, ROWS), BF16),
            pltpu.VMEM((PANEL, WIDE), F32),
            pltpu.VMEM((PANEL, ROWS), BF16),
            pltpu.VMEM((PANEL, WIDE), BF16),
            pltpu.VMEM((FEAT, WIDE), F32),
            pltpu.VMEM((WIDE, FEAT), BF16),
            pltpu.VMEM((FEAT, WIDE), BF16),
            pltpu.VMEM((ROWS, 128), I32),
            pltpu.VMEM((16, ROWS), I32),
            pltpu.VMEM((ROWS, 128), F32),
            pltpu.VMEM((NSUB * 16, ROWS), BF16),
            pltpu.VMEM((NSUB * 8, 128), F32),
            pltpu.VMEM((16, ROWS), F32),
            pltpu.VMEM((16, ROWS), F32),
            pltpu.VMEM((ROWS, ROWS), BF16),
            pltpu.VMEM((ROWS, ROWS), BF16),
            pltpu.VMEM((ROWS, 1), F32),
            pltpu.VMEM((FEAT, ROWS), F32),
            pltpu.VMEM((128, FEAT), BF16),
            pltpu.VMEM((128, FEAT), BF16),
            pltpu.VMEM((NXY * 8, 128), F32),
            pltpu.VMEM((32, 128), F32),
            pltpu.VMEM((PANEL, ROWS), BF16),
            pltpu.VMEM((FEAT, ROWS), F32),
            pltpu.VMEM((NZ, NXY * 16, FEAT), BF16),
            pltpu.VMEM((NZ, NXY * 16, FEAT), BF16),
            pltpu.VMEM((NZ * 16, FEAT), BF16),
            pltpu.VMEM((NZ * 16, FEAT), BF16),
            pltpu.VMEM((16, FEAT), F32),
            pltpu.VMEM((ROWS, FEAT), F32),
            pltpu.VMEM((ROWS, FEAT), F32),
            pltpu.SemaphoreType.DMA((5,)),
            sems(3), sems(NXY), sems(NXY), sems(NXY), sems(4), sems(NSUB), sems(NSUB), sems(NXY), sems(2),
            sems(NZ * NXY), sems(NZ),
        ],
        compiler_params=pltpu.CompilerParams(
            collective_id=0, has_side_effects=True, vmem_limit_bytes=54400 * 1024
        ),
    )(queries, keys, values, offsets.reshape(4, 128), negatives.T)
    dq, dk, dv, loss = pl.pallas_call(
        emit,
        out_shape=(wide, wide, wide, jax.ShapeDtypeStruct((1, 1), F32)),
        in_specs=[anywhere] * 3 + [vmem],
        out_specs=(anywhere, anywhere, anywhere, vmem),
        scratch_shapes=[pltpu.SemaphoreType.DMA((3,))],
        compiler_params=pltpu.CompilerParams(vmem_limit_bytes=1024 * 1024),
    )(*outs)
    return dq, dk, dv, loss.reshape(())


def solution(mesh):
    placed = (P("seq", "sub"), P("seq", "sub"), P("seq", "sub"), P("seq"), P("seq", None))
    return jax.shard_map(
        local,
        mesh=mesh,
        in_specs=placed,
        out_specs=(P("seq", "sub"), P("seq", "sub"), P("seq", "sub"), P()),
        check_vma=False,
    )
```

time: 77.4 us -> 70.2 us (0.907)
  the two profiles are of different devices: /device:TPU:28 before, /device:TPU:8 now
where the time goes in v2:
time: 70.2 us; the launch traced here: 69.9 us
  Pallas kernels  67.9 us (97%)
  local copies, waits for them, and re-layouts  1.43 us (2%)
    pallas_call x1, Pallas kernels, local(): pl.pallas_call(kernel, out_shape=(wide, wide, wide, jax.ShapeDtypeStruct(...  66.5 us
    unnamed x4, local copies, waits for them, and re-layouts  1.43 us
    pallas_call x1, Pallas kernels, local(): pl.pallas_call(emit, out_shape=(wide, wide, wide, jax.ShapeDtypeStruct((1...  1.41 us

profile of v2, /device:TPU:8, one launch (start us, length us, event | category | flops | bytes accessed | tf_op | source)
XLA Modules:
  0.0 69.9 jit_solution(10141028946811189034)
XLA Ops:
  0.6 0.0 copy-start.1
  0.6 0.7 copy-done.1
  1.3 0.0 copy-start
  1.3 0.8 %copy-done = s32[512,15]{0,1:T(8,128)S(1)} copy-done((s32[512,15]{0,1:T(8,128)S(1)}, s32[512,15]{0,1:T(8,128)}, u32[]{:S(2)}) %copy-start) | copy-done | bytes 30744
  2.1 66.5 %shard_map.84 = (bf16[512,256]{1,0:T(8,128)(2,1)S(1)}, bf16[512,256]{1,0:T(8,128)(2,1)S(1)}, bf16[512,256]{1,0:T(8,128)(2,1)S(1)}, f32[8,128]{1,0:T(8,128)S(1)}) custom-call(bf16[512,256]{1,0:T(8,128)(2,1)} %q_hbm.1, bf16[512,256]{1,0:T(8,128)(2,1)} %k_hbm.1, bf16[512,256]{1,0:T(8,128)(2,1)} %v_hbm.1, s32[4,128]{1,0:T(4,128)S(1)} %bitcast.4, ...), custom_call_target="tpu_custom_call" | custom-call | tf_op jit(solution)/shard_map/pallas_call | solution.py:598
  68.5 1.4 %shard_map.85 = (bf16[512,256]{1,0:T(8,128)(2,1)}, bf16[512,256]{1,0:T(8,128)(2,1)}, bf16[512,256]{1,0:T(8,128)(2,1)}, f32[1,1]{1,0:T(1,128)}) custom-call(bf16[512,256]{1,0:T(8,128)(2,1)S(1)} %get-tuple-element.12.dq, bf16[512,256]{1,0:T(8,128)(2,1)S(1)} %get-tuple-element.13.dk, bf16[512,256]{1,0:T(8,128)(2,1)S(1)} %get-tuple-element.14.dv, ...), custom_call_target="tpu_custom_call" | custom-call | tf_op jit(solution)/shard_map/pallas_call | solution.py:656
Async XLA Ops:
  0.6 0.7 copy-start.1
  1.3 0.8 %copy-start = (s32[512,15]{0,1:T(8,128)S(1)}, s32[512,15]{0,1:T(8,128)}, u32[]{:S(2)}) copy-start(s32[512,15]{0,1:T(8,128)} %param.9) | copy-start | bytes 92164

commit v3 on v2

--- a/solution.py
+++ b/solution.py
@@ -63,8 +63,8 @@
     dq_ref, dk_ref, dv_ref, loss_ref,
     q, k, v, off, neg, kx, vx, gat, kblk, vblk, kblk_t, vblk_t, k_t, v_t, s_scr, p1, p2, o1, att, att_t,
     idx, idx_t, picked, pk_buf, sq_buf, coef, rcoef, ct_hi, ct_lo, radial, grad_t,
-    tail_out, tail_in, loss_xy, loss_z, ds2, query2, gm, rs, rz_out, rz, own_term, dk_acc, dv_acc,
-    load_sem, z_sem, own_sem, low_sem, mid_sem, near_sem, pk_sem, sq_sem, lxy_sem, lz_sem, rs_sem, rz_sem,
+    tail_out, tail_in, loss_xy, loss_z, out1, out2, delta, k_part, v_part, ds2, query2, gm, rs, rz_out, rz, own_term, dk_acc, dv_acc,
+    load_sem, z_sem, own_sem, low_sem, mid_sem, near_sem, pk_sem, sq_sem, lxy_sem, lz_sem, rs_sem, plane_sem, rz_sem,
 ):
     seq = lax.axis_index("seq").astype(I32)
     sub = lax.axis_index("sub").astype(I32)
@@ -85,6 +85,11 @@
             src_ref=src, dst_ref=dst, send_sem=sems.at[0, j], recv_sem=sems.at[1, j],
             device_id=(to_seq, to_sub), device_id_type=MESH,
         )
+
+    def drain(ref, sems, i):
+        whole = remote(ref, ref, sems, i, prv, sub)
+        whole.wait_send()
+        whole.wait_recv()
 
     def each(count, make, act):
         def body(j, carry):
@@ -110,6 +115,7 @@
 
     gat[...] = jnp.zeros((NZ, NXY * 16, FEAT), BF16)
     rz[...] = jnp.zeros((NZ * 16, FEAT), BF16)
+    rs[z] = jnp.zeros((NXY * 16, FEAT), BF16)
     tail_in[...] = jnp.zeros((128, FEAT), BF16)
     barrier = pltpu.get_barrier_semaphore()
 
@@ -162,15 +168,15 @@
         return remote(tile, tile, z_sem, 2, z_seq(3), sub)
 
     def own_copy(j):
-        return remote(mine_tile, mine_tile, own_sem, j, xy_peer(j), sub)
+        return remote(mine_tile, mine_tile, own_sem, 0, xy_peer(j), sub)
 
     def low_copy(count):
         part = gat.at[pl.ds(0, count), own_rows, :]
-        return lambda j: remote(part, part, low_sem, j, xy_peer(j), sub)
+        return lambda j: remote(part, part, low_sem, 0, xy_peer(j), sub)
 
     def mid_copy(j):
         part = gat.at[2, own_rows, :]
-        return remote(part, part, mid_sem, j, xy_peer(j), sub)
+        return remote(part, part, mid_sem, 0, xy_peer(j), sub)
 
     @pl.when(z < 2)
     def _():
@@ -207,10 +213,10 @@
 
     @pl.when(z == 3)
     def _():
+        relay(3).wait_recv()
+        each(NXY, low_copy(2), start)
         third().wait_recv()
         each(NXY, mid_copy, start)
-        relay(3).wait_recv()
-        each(NXY, low_copy(2), start)
 
     loads[3].wait()
     loads[4].wait()
@@ -266,20 +272,21 @@
         l1[h] = jnp.concatenate([l1[h], jnp.sum(p, axis=0, keepdims=True)], axis=1)
         o1[cols, ROWS:WIDE] = tn(vx[:, cols], p.astype(BF16))
 
-    each(NXY, own_copy, finish)
+    others = pl.ds(0, (NXY - 1) * 16)
+    drain(gat.at[z, others, :], own_sem, 0)
 
     @pl.when(z == 1)
     def _():
-        each(NXY, low_copy(1), finish)
+        drain(gat.at[pl.ds(0, 1), others, :], low_sem, 0)
 
     @pl.when(z == 2)
     def _():
-        each(NXY, low_copy(2), finish)
+        drain(gat.at[pl.ds(0, 2), others, :], low_sem, 0)
 
     @pl.when(z == 3)
     def _():
-        each(NXY, mid_copy, finish)
-        each(NXY, low_copy(2), finish)
+        drain(gat.at[2, others, :], mid_sem, 0)
+        drain(gat.at[pl.ds(0, 2), others, :], low_sem, 0)
 
     in_first = (iota((256, DH), 0) & 15) < 8
     one = jnp.where(in_first, 1.0, 0.0).astype(BF16)
@@ -341,7 +348,7 @@
 
     def sq_copy(j):
         part = sq_buf.at[pl.ds(sq_row, 8), :]
-        return remote(part, part, sq_sem, j, seq, sub_peer(j))
+        return remote(part, part, sq_sem, 0, seq, sub_peer(j))
 
     each(NSUB, sq_copy, start)
     att[...] = att_t[...].T
@@ -366,10 +373,10 @@
 
     def pk_copy(j):
         part = pk_buf.at[pl.ds(pk_row, 16), :]
-        return remote(part, part, pk_sem, j, seq, sub_peer(j))
+        return remote(part, part, pk_sem, 0, seq, sub_peer(j))
 
     each(NSUB, pk_copy, start)
-    each(NSUB, sq_copy, finish)
+    drain(sq_buf.at[pl.ds(0, (NSUB - 1) * 8), :], sq_sem, 0)
     radius = jnp.sqrt(jnp.sum(sq_buf[...].reshape(NSUB, 8, 128), axis=0) / D + EPSILON)
     own_radius = jnp.concatenate([radius[b : b + 1, :] for b in range(4)], axis=1)
     parts = []
@@ -385,7 +392,7 @@
     factor = 1.0 / (D * TEMPER * own_radius * pair_radius)
     pair_share = 1.0 / (D * pair_radius * pair_radius)
     own_share = 1.0 / (D * own_radius * own_radius)
-    each(NSUB, pk_copy, finish)
+    drain(pk_buf.at[pl.ds(0, (NSUB - 1) * 16), :], pk_sem, 0)
     dots = jnp.sum(pk_buf[...].astype(F32).reshape(NSUB, 16, ROWS), axis=0)
 
     logits = dots * factor
@@ -417,7 +424,7 @@
 
     def lxy_copy(j):
         part = loss_xy.at[pl.ds(lxy_row, 8), :]
-        return remote(part, part, lxy_sem, j, xy_peer(j), sub)
+        return remote(part, part, lxy_sem, 0, xy_peer(j), sub)
 
     each(NXY, lxy_copy, start)
     row_c = iota((16, ROWS), 0)
@@ -432,69 +439,135 @@
             pairs = pairs + jnp.where(same, coef[k : k + 1, :], 0.0)
             pulls = pulls + jnp.where(same, rcoef[k : k + 1, :], 0.0)
         ct_hi[rows, :], ct_lo[rows, :] = split(pairs)
-        radial[rows, :] = jnp.sum(pulls, axis=1, keepdims=True)
+        radial[rows, :] = pulls[:, 0:128] + pulls[:, 128:256] + pulls[:, 256:384] + pulls[:, 384:512]
         return carry
 
     lax.fori_loop(0, ROWS // 16, table, 0)
     rows_own = att[0:ROWS, :]
+    radial_sum = jnp.sum(radial[...], axis=1, keepdims=True)
     cols_own = att_t[:, 0:ROWS]
-    pushed = nn(ct_hi[...], rows_own) + nn(ct_lo[...], rows_own) - radial[...] * rows_own.astype(F32)
+    pushed = nn(ct_hi[...], rows_own) + nn(ct_lo[...], rows_own) - radial_sum * rows_own.astype(F32)
     grad_t[...] = nn(cols_own, ct_hi[...]) + nn(cols_own, ct_lo[...]) - own_pull * cols_own.astype(F32) + pushed.T
     grad_t[:, late] += tn(ahead, far_hi) + tn(ahead, far_lo)
-    tail_copy.wait()
-    grad_t[:, 0:128] += tail_in[...].astype(F32).T
-
-    g1, g2, d1, d2 = [], [], [], []
-    for h in range(2):
-        cols = slice(h * DH, (h + 1) * DH)
-        grad = grad_t[cols, :]
-        wide = att_t[cols, 0:ROWS].astype(F32)
-        one, two = (grad * w1[h]).astype(BF16), (grad * w2[h]).astype(BF16)
-        g1.append(one)
-        g2.append(two)
-        d1.append(jnp.sum(one.astype(F32) * wide, axis=0, keepdims=True))
-        d2.append(jnp.sum(two.astype(F32) * wide, axis=0, keepdims=True))
-    both2 = jnp.concatenate(g2, axis=0)
-    d16 = jnp.concatenate([jnp.broadcast_to(d2[0], (8, ROWS)), jnp.broadcast_to(d2[1], (8, ROWS))], axis=0)
+    def scale(span):
+        for h in range(2):
+            cols = slice(h * DH, (h + 1) * DH)
+            grad = grad_t[cols, span]
+            wide = att_t[cols, span].astype(F32)
+            one, two = (grad * w1[h][:, span]).astype(BF16), (grad * w2[h][:, span]).astype(BF16)
+            out1[cols, span] = one
+            out2[cols, span] = two
+            delta[h : h + 1, span] = jnp.sum(one.astype(F32) * wide, axis=0, keepdims=True)
+            delta[2 + h : 3 + h, span] = jnp.sum(two.astype(F32) * wide, axis=0, keepdims=True)
 
     def rows256(w):
         return pl.ds(pl.multiple_of(w * 256, 256), 256)
 
-    def rs_copy(w):
+    def part(w, span, d16):
+        rows = rows256(w)
+        count = span.stop - span.start
+        s_scr[0:256, span] = nn(vblk[rows, :], out2[:, span])
+
+        def slope(i, carry):
+            x = s_scr[rows64(i), span].reshape(4, 16, count) - d16[None]
+            here = rows64(i, w * 256)
+            p = p2[here, span].astype(F32).reshape(4, 16, count)
+            ds2[here, span] = (x * p).reshape(64, count).astype(BF16)
+            return carry
+
+        lax.fori_loop(0, 4, slope, 0)
+        return nn(ds2[rows, span], q[span, :]), nt(p2[rows, span], out2[:, span])
+
+    def both_heads(span):
+        count = span.stop - span.start
+        return jnp.concatenate(
+            [jnp.broadcast_to(delta[2:3, span], (8, count)), jnp.broadcast_to(delta[3:4, span], (8, count))], axis=0
+        )
+
+    most, few = slice(128, ROWS), slice(0, 128)
+    scale(most)
+    d_most = both_heads(most)
+
+    def most_part(w, carry):
+        rows = rows256(w)
+        k_part[rows, :], v_part[rows, :] = part(w, most, d_most)
+        return carry
+
+    lax.fori_loop(0, z + 1, most_part, 0)
+    tail_copy.wait()
+    grad_t[:, few] += tail_in[...].astype(F32).T
+    scale(few)
+    d_few = both_heads(few)
+
+    def rs_copy(w, sems, slot):
         def make(j):
             to = pl.ds(pl.multiple_of(lax.rem(xy + j, NXY) * 16, 16), 16)
-            return remote(gm.at[w, to, :], rs.at[w, own_rows, :], rs_sem, w * NXY + j, xy_peer(j), sub)
+            return remote(gm.at[w, to, :], rs.at[w, own_rows, :], sems, slot(j), xy_peer(j), sub)
 
         return make
 
     def wave(w, carry):
         rows = rows256(w)
-        s_scr[0:256, 0:ROWS] = nn(vblk[rows, :], both2)
-
-        def slope(i, carry):
-            x = s_scr[rows64(i), 0:ROWS].reshape(4, 16, ROWS) - d16[None]
-            here = rows64(i, w * 256)
-            p = p2[here, 0:ROWS].astype(F32).reshape(4, 16, ROWS)
-            ds2[here, :] = (x * p).reshape(64, ROWS).astype(BF16)
-            return carry
-
-        lax.fori_loop(0, 4, slope, 0)
+        key2, value2 = part(w, few, d_few)
+        key2 = key2 + k_part[rows, :]
+        value2 = value2 + v_part[rows, :]
         head0 = (iota((256, DH), 0) & 15) < 8
-        key2 = nn(ds2[rows, :], q[0:ROWS, :])
-        value2 = nt(p2[rows, 0:ROWS], both2)
         gm[w, :, 0:DH] = (jnp.where(head0, key2[:, :DH], key2[:, DH:]) * SCALE).astype(BF16)
         gm[w, :, DH:FEAT] = jnp.where(head0, value2[:, :DH], value2[:, DH:]).astype(BF16)
-        each(NXY, rs_copy(w), start)
+
         rs[w, own_rows, :] = gm[w, own_rows, :]
+
+        @pl.when(w < z)
+        def _():
+            each(NXY, rs_copy(w, rs_sem, lambda j: w), start)
+
         return carry
 
     lax.fori_loop(0, z + 1, wave, 0)
 
-    each(NXY, lxy_copy, finish)
-    plane_loss = jnp.sum(loss_xy[...].reshape(NXY, 8, 128), axis=0)
-    loss_z[0:8, :] = plane_loss
-    lz_first = remote(loss_z.at[pl.ds(0, 8), :], loss_z.at[pl.ds(8, 8), :], lz_sem, 0, z_seq(z + 1 - 2 * lax.rem(z, 2)), sub)
-    lz_first.start()
+    plane_copy = rs_copy(z, plane_sem, lambda j: j)
+
+    def send(j, carry):
+        plane_copy(j).start()
+        return carry
+
+    lax.fori_loop(NXY - xy, NXY, send, 0)
+
+    drain(loss_xy.at[pl.ds(0, (NXY - 1) * 8), :], lxy_sem, 0)
+    plane_row = pl.ds(pl.multiple_of(z * 8, 8), 8)
+    loss_z[plane_row, :] = jnp.sum(loss_xy[...].reshape(NXY, 8, 128), axis=0)
+
+    def loss_swap():
+        part = loss_z.at[plane_row, :]
+        return remote(part, part, lz_sem, 0, z_seq(1 - z), sub)
+
+    def loss_pair(to):
+        part = loss_z.at[pl.ds(0, 16), :]
+        return remote(part, part, lz_sem, 1, z_seq(to), sub)
+
+    def loss_one(w, i, to):
+        part = loss_z.at[pl.ds(w * 8, 8), :]
+        return remote(part, part, lz_sem, i, z_seq(to), sub)
+
+    def from2():
+        return [loss_one(2, 2, 0), loss_one(2, 3, 1), loss_one(2, 4, 3)]
+
+    def from3():
+        return [loss_one(3, 5, 0), loss_one(3, 6, 1), loss_one(3, 7, 2)]
+
+    @pl.when(z < 2)
+    def _():
+        loss_swap().start()
+
+    @pl.when(z == 2)
+    def _():
+        for copy in from2():
+            copy.start()
+
+    @pl.when(z == 3)
+    def _():
+        for copy in from3():
+            copy.start()
 
     query2[...] = jnp.zeros((FEAT, ROWS), F32)
 
@@ -506,10 +579,10 @@
     for h in range(2):
         cols = slice(h * DH, (h + 1) * DH)
         base = h * ROWS
-        s_scr[base : base + ROWS, 0:ROWS] = nn(v[:, cols], g1[h])
-
-        def slope1(i, carry, base=base, shift=d1[h]):
-            x = s_scr[rows64(i, base), 0:ROWS] - shift
+        s_scr[base : base + ROWS, 0:ROWS] = nn(v[:, cols], out1[cols, :])
+
+        def slope1(i, carry, base=base, h=h):
+            x = s_scr[rows64(i, base), 0:ROWS] - delta[h : h + 1, :]
             s_scr[rows64(i, base), 0:ROWS] = x * p1[rows64(i, base), :].astype(F32)
             return carry
 
@@ -518,12 +591,11 @@
         query = (nn(k_t[cols, :], close) + query2[cols, :]) * SCALE
         dq_ref[:, cols] = query.T.astype(BF16)
         dk_acc[:, cols] = nn(close, q[0:ROWS, cols]) * SCALE
-        dv_acc[:, cols] = nt(p1[base : base + ROWS, :], g1[h])
+        dv_acc[:, cols] = nt(p1[base : base + ROWS, :], out1[cols, :])
     dk_ref[...] = dk_acc[...].astype(BF16)
     dv_ref[...] = dv_acc[...].astype(BF16)
 
     def plane_sum(w):
-        each(NXY, rs_copy(w), finish)
         return jnp.sum(rs[w].astype(F32).reshape(NXY, 16, FEAT), axis=0)
 
     rz_row = pl.multiple_of(z * 16, 16)
@@ -533,16 +605,33 @@
         return remote(rz_out.at[part, :], rz.at[pl.ds(rz_row, 16), :], rz_sem, z - w, z_seq(w), sub)
 
     def down(w, carry):
+        drain(rs.at[w, others, :], rs_sem, w)
         rz_out[pl.ds(pl.multiple_of(w * 16, 16), 16), :] = plane_sum(w).astype(BF16)
         rz_copy(w).start()
         return carry
 
     lax.fori_loop(0, z, down, 0)
+    def plane_sent(j, carry):
+        plane_copy(j).wait_send()
+        return carry
+
+    def plane_came(j, carry):
+        plane_copy(j).wait_recv()
+        return carry
+
+    lax.fori_loop(xy + 1, NXY, plane_came, 0)
+    lax.fori_loop(NXY - xy, NXY, plane_sent, 0)
     own_term[...] = plane_sum(z)
-    lz_first.wait()
-    loss_z[16:24, :] = loss_z[0:8, :] + loss_z[8:16, :]
-    lz_second = remote(loss_z.at[pl.ds(16, 8), :], loss_z.at[pl.ds(24, 8), :], lz_sem, 1, z_seq(3 - z), sub)
-    lz_second.start()
+
+    @pl.when(z == 0)
+    def _():
+        loss_swap().wait()
+        loss_pair(3).start()
+
+    @pl.when(z == 1)
+    def _():
+        loss_swap().wait()
+        loss_pair(2).start()
 
     def sent(w, carry):
         rz_copy(w).wait_send()
@@ -563,8 +652,34 @@
         for acc, ref, lanes in ((dk_acc, dk_ref, slice(0, DH)), (dv_acc, dv_ref, slice(DH, FEAT))):
             extra = jnp.concatenate([term[i : i + 1, lanes], term[8 + i : 9 + i, lanes]], axis=1)
             ref[rows, :] = (acc[rows, :] + jnp.where(last, extra, 0.0)).astype(BF16)
-    lz_second.wait()
-    loss_ref[...] = loss_z[16:24, :] + loss_z[24:32, :]
+
+    @pl.when(z == 0)
+    def _():
+        loss_pair(3).wait_send()
+        loss_one(2, 2, 0).wait_recv()
+        loss_one(3, 5, 0).wait_recv()
+
+    @pl.when(z == 1)
+    def _():
+        loss_pair(2).wait_send()
+        loss_one(2, 3, 1).wait_recv()
+        loss_one(3, 6, 1).wait_recv()
+
+    @pl.when(z == 2)
+    def _():
+        for copy in from2():
+            copy.wait_send()
+        loss_pair(2).wait_recv()
+        loss_one(3, 7, 2).wait_recv()
+
+    @pl.when(z == 3)
+    def _():
+        for copy in from3():
+            copy.wait_send()
+        loss_pair(3).wait_recv()
+        loss_one(2, 4, 3).wait_recv()
+
+    loss_ref[...] = jnp.sum(loss_z[...].reshape(NZ, 8, 128), axis=0)
 
     @pl.when(z < 2)
     def _():
@@ -630,12 +745,17 @@
             pltpu.VMEM((16, ROWS), F32),
             pltpu.VMEM((ROWS, ROWS), BF16),
             pltpu.VMEM((ROWS, ROWS), BF16),
-            pltpu.VMEM((ROWS, 1), F32),
+            pltpu.VMEM((ROWS, 128), F32),
             pltpu.VMEM((FEAT, ROWS), F32),
             pltpu.VMEM((128, FEAT), BF16),
             pltpu.VMEM((128, FEAT), BF16),
             pltpu.VMEM((NXY * 8, 128), F32),
-            pltpu.VMEM((32, 128), F32),
+            pltpu.VMEM((NZ * 8, 128), F32),
+            pltpu.VMEM((FEAT, ROWS), BF16),
+            pltpu.VMEM((FEAT, ROWS), BF16),
+            pltpu.VMEM((8, ROWS), F32),
+            pltpu.VMEM((PANEL, FEAT), F32),
+            pltpu.VMEM((PANEL, FEAT), F32),
             pltpu.VMEM((PANEL, ROWS), BF16),
             pltpu.VMEM((FEAT, ROWS), F32),
             pltpu.VMEM((NZ, NXY * 16, FEAT), BF16),
@@ -646,8 +766,8 @@
             pltpu.VMEM((ROWS, FEAT), F32),
             pltpu.VMEM((ROWS, FEAT), F32),
             pltpu.SemaphoreType.DMA((5,)),
-            sems(3), sems(NXY), sems(NXY), sems(NXY), sems(4), sems(NSUB), sems(NSUB), sems(NXY), sems(2),
-            sems(NZ * NXY), sems(NZ),
+            sems(3), sems(1), sems(1), sems(1), sems(4), sems(1), sems(1), sems(1), sems(8),
+            sems(NZ - 1), sems(NXY), sems(NZ),
         ],
         compiler_params=pltpu.CompilerParams(
             collective_id=0, has_side_effects=True, vmem_limit_bytes=54400 * 1024

time: 70.2 us -> 66.8 us (0.952)
  the two profiles are of different devices: /device:TPU:8 before, /device:TPU:128 now
where the time goes in v3:
time: 66.8 us; the launch traced here: 66.5 us
  Pallas kernels  64.5 us (97%)
  local copies, waits for them, and re-layouts  1.43 us (2%)
    pallas_call x1, Pallas kernels, local(): pl.pallas_call(kernel, out_shape=(wide, wide, wide, jax.ShapeDtypeStruct(...  63 us
    unnamed x4, local copies, waits for them, and re-layouts  1.43 us
    pallas_call x1, Pallas kernels, local(): pl.pallas_call(emit, out_shape=(wide, wide, wide, jax.ShapeDtypeStruct((1...  1.41 us

profile of v3, /device:TPU:128, one launch (start us, length us, event | category | flops | bytes accessed | tf_op | source)
XLA Modules:
  0.0 66.5 jit_solution(2701649594450088314)
XLA Ops:
  0.6 0.0 copy-start.1
  0.6 0.7 %copy-done.1 = s32[512]{0:T(512)S(1)} copy-done((s32[512]{0:T(512)S(1)}, s32[512]{0:T(512)}, u32[]{:S(2)}) %copy-start.1) | copy-done | bytes 2072
  1.3 0.0 copy-start
  1.3 0.8 %copy-done = s32[512,15]{0,1:T(8,128)S(1)} copy-done((s32[512,15]{0,1:T(8,128)S(1)}, s32[512,15]{0,1:T(8,128)}, u32[]{:S(2)}) %copy-start) | copy-done | bytes 30744
  2.1 63.0 %shard_map.84 = (bf16[512,256]{1,0:T(8,128)(2,1)S(1)}, bf16[512,256]{1,0:T(8,128)(2,1)S(1)}, bf16[512,256]{1,0:T(8,128)(2,1)S(1)}, f32[8,128]{1,0:T(8,128)S(1)}) custom-call(bf16[512,256]{1,0:T(8,128)(2,1)} %q_hbm.1, bf16[512,256]{1,0:T(8,128)(2,1)} %k_hbm.1, bf16[512,256]{1,0:T(8,128)(2,1)} %v_hbm.1, s32[4,128]{1,0:T(4,128)S(1)} %bitcast.4, ...), custom_call_target="tpu_custom_call" | custom-call | tf_op jit(solution)/shard_map/pallas_call | solution.py:713
  65.1 1.4 %shard_map.85 = (bf16[512,256]{1,0:T(8,128)(2,1)}, bf16[512,256]{1,0:T(8,128)(2,1)}, bf16[512,256]{1,0:T(8,128)(2,1)}, f32[1,1]{1,0:T(1,128)}) custom-call(bf16[512,256]{1,0:T(8,128)(2,1)S(1)} %get-tuple-element.12.dq, bf16[512,256]{1,0:T(8,128)(2,1)S(1)} %get-tuple-element.13.dk, bf16[512,256]{1,0:T(8,128)(2,1)S(1)} %get-tuple-element.14.dv, ...), custom_call_target="tpu_custom_call" | custom-call | tf_op jit(solution)/shard_map/pallas_call | solution.py:776
Async XLA Ops:
  0.6 0.7 %copy-start.1 = (s32[512]{0:T(512)S(1)}, s32[512]{0:T(512)}, u32[]{:S(2)}) copy-start(s32[512]{0:T(512)} %param.8) | copy-start | bytes 6148
  1.3 0.8 %copy-start = (s32[512,15]{0,1:T(8,128)S(1)}, s32[512,15]{0,1:T(8,128)}, u32[]{:S(2)}) copy-start(s32[512,15]{0,1:T(8,128)} %param.9) | copy-start | bytes 92164

commit v4 on v3

--- a/solution.py
+++ b/solution.py
@@ -59,9 +59,9 @@
 
 
 def kernel(
-    q_hbm, k_hbm, v_hbm, off_hbm, neg_hbm,
+    q_hbm, k_hbm, v_hbm, off_hbm,
     dq_ref, dk_ref, dv_ref, loss_ref,
-    q, k, v, off, neg, kx, vx, gat, kblk, vblk, kblk_t, vblk_t, k_t, v_t, s_scr, p1, p2, o1, att, att_t,
+    q, k, v, off, kx, vx, gat, kblk, vblk, kblk_t, vblk_t, k_t, v_t, s_scr, p1, p2, o1, att, att_t,
     idx, idx_t, picked, pk_buf, sq_buf, coef, rcoef, ct_hi, ct_lo, radial, grad_t,
     tail_out, tail_in, loss_xy, loss_z, out1, out2, delta, k_part, v_part, ds2, query2, gm, rs, rz_out, rz, own_term, dk_acc, dv_acc,
     load_sem, z_sem, own_sem, low_sem, mid_sem, near_sem, pk_sem, sq_sem, lxy_sem, lz_sem, rs_sem, plane_sem, rz_sem,
@@ -107,7 +107,7 @@
     loads = [
         pltpu.make_async_copy(src, dst, load_sem.at[i])
         for i, (src, dst) in enumerate(
-            [(k_hbm, k), (v_hbm, v), (q_hbm, q.at[pl.ds(0, ROWS), :]), (off_hbm, off), (neg_hbm, neg)]
+            [(k_hbm, k), (v_hbm, v), (q_hbm, q.at[pl.ds(0, ROWS), :]), (off_hbm, off)]
         )
     ]
     for load in loads:
@@ -219,13 +219,12 @@
         each(NXY, mid_copy, start)
 
     loads[3].wait()
-    loads[4].wait()
     k_t[...] = k[...].T
     v_t[...] = v[...].T
-    idx_t[0:15, :] = neg[...]
+    idx_t[0:15, :] = off[0:15, :]
     for b in range(4):
         cols = slice(b * 128, (b + 1) * 128)
-        idx_t[15:16, cols] = off[b : b + 1, :] + iota((1, 128), 1) + b * 128
+        idx_t[15:16, cols] = off[15:16, cols] + iota((1, 128), 1) + b * 128
     for b in range(4):
         cols = slice(b * 128, (b + 1) * 128)
         idx[cols, :] = jnp.concatenate([idx_t[:, cols], jnp.zeros((112, 128), I32)], axis=0).T
@@ -285,7 +284,6 @@
 
     @pl.when(z == 3)
     def _():
-        drain(gat.at[2, others, :], mid_sem, 0)
         drain(gat.at[pl.ds(0, 2), others, :], low_sem, 0)
 
     in_first = (iota((256, DH), 0) & 15) < 8
@@ -294,7 +292,13 @@
     in_first_t = (iota((DH, 256), 1) & 15) < 8
     one_t = jnp.where(in_first_t, 1.0, 0.0).astype(BF16)
     two_t = jnp.where(in_first_t, 0.0, 1.0).astype(BF16)
-    for b in range(NZ):
+    for b in (0, 1, 3, 2):
+        if b == 2:
+
+            @pl.when(z == 3)
+            def _():
+                drain(gat.at[2, others, :], mid_sem, 0)
+
         rows = slice(b * 256, (b + 1) * 256)
         for lanes, blk, blk_t in ((slice(0, DH), kblk, kblk_t), (slice(DH, FEAT), vblk, vblk_t)):
             tile = gat[b, :, lanes]
@@ -303,8 +307,8 @@
             blk[rows, DH:FEAT] = tile * two
             blk_t[0:DH, rows] = tile_t * one_t
             blk_t[DH:FEAT, rows] = tile_t * two_t
-
-    s_scr[...] = nt(kblk[...], q[...])
+        s_scr[rows, :] = nt(kblk[rows, :], q[...])
+
     slab = lax.shift_right_logical(iota((64, WIDE), 0), 4)
     limit = jnp.where(iota((1, WIDE), 1) < ROWS, seq, nxt)
 
@@ -713,14 +717,13 @@
     outs = pl.pallas_call(
         kernel,
         out_shape=(wide, wide, wide, jax.ShapeDtypeStruct((8, 128), F32)),
-        in_specs=[anywhere] * 5,
+        in_specs=[anywhere] * 4,
         out_specs=(vmem,) * 4,
         scratch_shapes=[
             pltpu.VMEM((WIDE, FEAT), BF16),
             pltpu.VMEM((ROWS, FEAT), BF16),
             pltpu.VMEM((ROWS, FEAT), BF16),
-            pltpu.VMEM((4, 128), I32),
-            pltpu.VMEM((15, ROWS), I32),
+            pltpu.VMEM((16, ROWS), I32),
             pltpu.VMEM((OFFMAX, FEAT), BF16),
             pltpu.VMEM((OFFMAX, FEAT), BF16),
             pltpu.VMEM((NZ, NXY * 16, FEAT), BF16),
@@ -765,14 +768,14 @@
             pltpu.VMEM((16, FEAT), F32),
             pltpu.VMEM((ROWS, FEAT), F32),
             pltpu.VMEM((ROWS, FEAT), F32),
-            pltpu.SemaphoreType.DMA((5,)),
+            pltpu.SemaphoreType.DMA((4,)),
             sems(3), sems(1), sems(1), sems(1), sems(4), sems(1), sems(1), sems(1), sems(8),
             sems(NZ - 1), sems(NXY), sems(NZ),
         ],
         compiler_params=pltpu.CompilerParams(
             collective_id=0, has_side_effects=True, vmem_limit_bytes=54400 * 1024
         ),
-    )(queries, keys, values, offsets.reshape(4, 128), negatives.T)
+    )(queries, keys, values, jnp.concatenate([negatives.T, offsets[None, :]], axis=0))
     dq, dk, dv, loss = pl.pallas_call(
         emit,
         out_shape=(wide, wide, wide, jax.ShapeDtypeStruct((1, 1), F32)),

time: 66.8 us -> 66.1 us (0.990)
  other arithmetic: 0 us -> 0.77 us
  local copies, waits for them, and re-layouts: 1.43 us -> 0.67 us
  Pallas kernels: 64.5 us -> 63.8 us
    concatenate x0 -> x1, other arithmetic: none -> 0.77 us  [local(): jnp.concatenate([negatives.T, offsets[None, :]], axis=0)]
    unnamed x4 -> x2, local copies, waits for them, and re-layouts: 1.43 us -> 0.67 us
where the time goes in v4:
time: 66.1 us; the launch traced here: 65.9 us
  Pallas kernels  63.8 us (97%)
  other arithmetic  0.77 us (1%)
  local copies, waits for them, and re-layouts  0.67 us (1%)
    pallas_call x1, Pallas kernels, local(): pl.pallas_call(kernel, out_shape=(wide, wide, wide, jax.ShapeDtypeStruct(...  62.4 us
    pallas_call x1, Pallas kernels, local(): pl.pallas_call(emit, out_shape=(wide, wide, wide, jax.ShapeDtypeStruct((1...  1.41 us

profile of v4, /device:TPU:128, one launch (start us, length us, event | category | flops | bytes accessed | tf_op | source)
XLA Modules:
  0.0 65.9 jit_solution(9849499236808007548)
XLA Ops:
  0.6 0.0 copy-start
  0.6 0.7 %copy-done = s32[512]{0:T(512)S(1)} copy-done((s32[512]{0:T(512)S(1)}, s32[512]{0:T(512)}, u32[]{:S(2)}) %copy-start) | copy-done | bytes 2072
  1.3 0.8 %pad_add_fusion.off_hbm = s32[16,512]{1,0:T(8,128)S(1)} fusion(s32[1,512]{1,0:T(1,128)S(1)} %bitcast.4, s32[15,512]{1,0:T(8,128)} %bitcast.3), kind=kLoop, calls=%fused_computation | loop fusion | flops 8192 | bytes 65536 | tf_op jit(solution)/shard_map/concatenate | solution.py:778
  2.1 62.4 %shard_map.84 = (bf16[512,256]{1,0:T(8,128)(2,1)S(1)}, bf16[512,256]{1,0:T(8,128)(2,1)S(1)}, bf16[512,256]{1,0:T(8,128)(2,1)S(1)}, f32[8,128]{1,0:T(8,128)S(1)}) custom-call(bf16[512,256]{1,0:T(8,128)(2,1)} %q_hbm.1, bf16[512,256]{1,0:T(8,128)(2,1)} %k_hbm.1, bf16[512,256]{1,0:T(8,128)(2,1)} %v_hbm.1, s32[16,512]{1,0:T(8,128)S(1)} %pad_add_fusion.off_hbm), custom_call_target="tpu_custom_call" | custom-call | tf_op jit(solution)/shard_map/pallas_call | solution.py:717
  64.5 1.4 %shard_map.85 = (bf16[512,256]{1,0:T(8,128)(2,1)}, bf16[512,256]{1,0:T(8,128)(2,1)}, bf16[512,256]{1,0:T(8,128)(2,1)}, f32[1,1]{1,0:T(1,128)}) custom-call(bf16[512,256]{1,0:T(8,128)(2,1)S(1)} %get-tuple-element.12.dq, bf16[512,256]{1,0:T(8,128)(2,1)S(1)} %get-tuple-element.13.dk, bf16[512,256]{1,0:T(8,128)(2,1)S(1)} %get-tuple-element.14.dv, ...), custom_call_target="tpu_custom_call" | custom-call | tf_op jit(solution)/shard_map/pallas_call | solution.py:779
Async XLA Ops:
  0.6 0.7 %copy-start = (s32[512]{0:T(512)S(1)}, s32[512]{0:T(512)}, u32[]{:S(2)}) copy-start(s32[512]{0:T(512)} %param.8) | copy-start | bytes 6148
